TPU v7x, 768 devices: a whole 4x8x12 slice. The times are simulated.
768 devices in a mesh: dp: 64 (over y, z_hi, core), blk: 12 (over z_lo, x).
Axes of the slice: x: 4, y: 8, z: 12 (z_hi: 4, z_lo: 3; z = z_hi * 3 + z_lo), core: 2. Of those that a mesh axis runs over, the one named last changes fastest.
Arguments:
- tokens: bfloat16 [98304, 6144], P('dp', 'blk'), may hold values from -6 to 6
- key_grad: bfloat16 [98304, 512], P(('dp', 'blk')), may hold values from -6 to 6
- weight: float32 [6144, 512], P('blk'), may hold values from -6 to 6
- moment: float32 [6144, 512], P('blk'), may hold values from -6 to 6
- second: float32 [6144, 512], P('blk'), may hold values from 0.5 to 20
Outputs:
- keys: bfloat16 [98304, 512], P(('dp', 'blk'))
- token_grad: bfloat16 [98304, 6144], P('dp', 'blk')
- weight_grad: float32 [6144, 512], P('blk')
- weight_new: float32 [6144, 512], P('blk')
- moment_new: float32 [6144, 512], P('blk')
- second_new: float32 [6144, 512], P('blk')
All inputs are finite; a program needn't handle non-finite values.
Results may differ from a plain program's by a relative error of at most 0.0049.
Values may be sent and summed in bfloat16 or wider, within the bound.
No kernel may reach another device: no remote copies, remote signals or barrier semaphores. Data moves between devices by JAX's collectives and lax.ppermute only.
A program may use at most 64 MiB of HBM per device.

v0:
```python
import jax
import jax.numpy as jnp
from jax import lax
from jax.sharding import PartitionSpec as P

D = 6144
STEP = 100


def optimize(weight, moment, second, weight_grad):
    moment_new = 0.9 * moment + 0.1 * weight_grad
    second_new = 0.999 * second + 0.001 * weight_grad * weight_grad
    first_fix = 1.0 - 0.9**STEP
    second_fix = 1.0 - 0.999**STEP
    step_dir = moment_new / first_fix / (jnp.sqrt(second_new / second_fix) + 1e-08)
    weight_new = weight - 0.05 * (step_dir + 0.1 * weight)
    return (weight_new, moment_new, second_new)


def local(tokens, key_grad, weight, moment, second):
    factor = D ** (-0.5)
    scaled = (weight * factor).astype(jnp.bfloat16)
    own_rows = key_grad.shape[0]
    partial_value = jnp.dot(tokens, scaled, preferred_element_type=jnp.float32)
    summed = lax.psum(partial_value, "blk")
    first_row = lax.axis_index("blk") * own_rows
    keys = lax.dynamic_slice_in_dim(summed, first_row, own_rows, 0).astype(jnp.bfloat16)
    piece = lax.all_gather(key_grad, "blk", axis=0, tiled=True)
    grad_total = lax.dot_general(
        tokens, piece, (((0,), (0,)), ((), ())), preferred_element_type=jnp.float32
    )
    back = lax.dot_general(
        piece, scaled, (((1,), (1,)), ((), ())), preferred_element_type=jnp.float32
    ).astype(jnp.bfloat16)
    local_grad = grad_total
    local_grad = local_grad * factor
    weight_grad = lax.psum(local_grad, "dp")
    weight_new, moment_new, second_new = optimize(weight, moment, second, weight_grad)
    return (keys, back, weight_grad, weight_new, moment_new, second_new)


def solution(mesh):
    in_specs = (
        P("dp", "blk"),
        P(("dp", "blk"), None),
        P("blk", None),
        P("blk", None),
        P("blk", None),
    )
    out_specs = (
        P(("dp", "blk"), None),
        P("dp", "blk"),
        P("blk", None),
        P("blk", None),
        P("blk", None),
        P("blk", None),
    )
    return jax.shard_map(local, mesh=mesh, in_specs=in_specs, out_specs=out_specs, check_vma=False)
```

profile of v0, /device:TPU:1, one launch (start us, length us, event | category | flops | bytes accessed | tf_op | source)
XLA Modules:
  0.0 728.3 jit_solution(10386060232075557979)
XLA Ops:
  7.2 0.0 copy-start
  7.2 0.0 all-gather.2.cloned.1.call-start
  7.2 0.7 all-gather.2.cloned.1.call-update
  7.9 0.0 all-reduce.3.cloned.1.call-start
  8.0 0.6 copy-done
  8.6 3.9 convolution_bitcast_fusion
  12.5 63.6 %all-gather.2.cloned.1.call-done = bf16[1536,512]{1,0:T(8,128)(2,1)} async-done(((bf16[128,512]{1,0:T(8,128)(2,1)}), bf16[1536,512]{1,0:T(8,128)(2,1)}) %all-gather.2.cloned.1.call-update) | async-done | bytes 1572880 | tf_op jit(solution)/shard_map/all_gather | solution.py:28
  76.1 3.4 convolution_multiply_fusion
  79.5 0.0 all-reduce.3.cloned.1.call-update
  79.5 0.0 copy-start.1
  79.5 74.8 %all-reduce.4 = bf16[1536,512]{0,1:T(8,128)(2,1)} all-reduce(f32[1536,512]{0,1:T(8,128)} %convolution_bitcast_fusion), channel_id=1, replica_groups=mesh['dp'=64,'blk'=12] {'blk'}, use_global_device_ids=true, to_apply=%region_0.0 | all-reduce | flops 786432 | bytes 4718592 | tf_op jit(solution)/shard_map/psum | solution.py:25
  154.3 0.9 dynamic-slice_convert_fusion
  155.2 0.8 copy.11
  156.0 0.0 copy-done.1
  156.0 3.6 fusion
  159.6 2.6 copy.12
  162.2 554.1 %all-reduce.3.cloned.1.call-done = f32[512,512]{1,0:T(8,128)} async-done(((f32[512,512]{1,0:T(8,128)}), f32[512,512]{1,0:T(8,128)}) %all-reduce.3.cloned.1.call-update) | async-done | bytes 1048592 | tf_op jit(solution)/shard_map/psum | solution.py:37
  716.3 0.0 copy-start.2
  716.3 4.2 multiply_subtract_fusion
  720.5 0.0 copy-done.2
  720.5 1.0 copy.16
Async XLA Ops:
  7.2 1.4 copy-start
  7.2 68.9 %all-gather.2.cloned.1.call-start = ((), (), s32[]{:S(2)}) async-start(), calls=%async_computation | async-start | bytes 1703936 | tf_op jit(solution)/shard_map/all_gather | solution.py:28
  7.9 708.4 %all-reduce.3.cloned.1.call-start = ((), (), s32[]{:S(2)}) async-start(), calls=%async_computation.1 | async-start | bytes 2097152 | tf_op jit(solution)/shard_map/psum | solution.py:37
  79.5 76.5 %copy-start.1 = (f32[512,512]{1,0:T(8,128)S(1)}, f32[512,512]{1,0:T(8,128)}, u32[]{:S(2)}) copy-start(f32[512,512]{1,0:T(8,128)} %param.7) | copy-start | bytes 3145732
  716.3 4.2 copy-start.2
Sparse Core Ops, SparseCore 0:
  10.4 65.6 all-gather.1
  79.9 636.4 all-reduce.2
where the time goes:
time: 730 us; the launch traced here: 728 us
  waiting for transfers between devices  618 us (85%)
  blocking collectives  74.8 us (10%)
  between operations  14.1 us (2%)
  matrix products  10.9 us (1%)
    psum x1, waiting for transfers between devices, local(): weight_grad = lax.psum(local_grad, 'dp')  554 us
    psum x1, blocking collectives, local(): summed = lax.psum(partial_value, 'blk')  74.8 us
    all_gather x1, waiting for transfers between devices, local(): piece = lax.all_gather(key_grad, 'blk', axis=0, tiled=True)  63.6 us
  transfers between devices with their start and end apart: 2, of which 2 were waited for; matrix products, arithmetic and copies ran while one was open for 2% of the time, Pallas kernels for 0%

commit v1 on v0

v1 whole, which is shorter than its diff:
```python
import jax
import jax.numpy as jnp
from jax import lax
from jax.experimental import pallas as pl
from jax.experimental.pallas import tpu as pltpu
from jax.sharding import Mesh, PartitionSpec as P

D = 6144
STEP = 100
FACTOR = D ** (-0.5)
AXES = ("y", "zh", "c", "zl", "x")
DP = ("y", "zh", "c")
BLK = ("zl", "x")
PAIR = ("c", "y")
BF16, F32 = jnp.bfloat16, jnp.float32
VMEM = pl.BlockSpec(memory_space=pltpu.VMEM)
SMEM = pl.BlockSpec(memory_space=pltpu.SMEM)
ANY = pl.BlockSpec(memory_space=pl.ANY)


def optimize(weight, moment, second, weight_grad):
    moment_new = 0.9 * moment + 0.1 * weight_grad
    second_new = 0.999 * second + 0.001 * weight_grad * weight_grad
    first_fix = 1.0 - 0.9**STEP
    second_fix = 1.0 - 0.999**STEP
    step_dir = moment_new / first_fix / (jnp.sqrt(second_new / second_fix) + 1e-08)
    weight_new = weight - 0.05 * (step_dir + 0.1 * weight)
    return (weight_new, moment_new, second_new)


def params(mib):
    return pltpu.CompilerParams(vmem_limit_bytes=mib << 20)


def cost(flops, nbytes):
    return pl.CostEstimate(flops=flops, bytes_accessed=nbytes, transcendentals=0)


def like(shape, dtype=BF16):
    return jax.ShapeDtypeStruct(shape, dtype)


def swap_parts(x, axes):
    return lax.all_to_all(x, axes, 0, 0, tiled=True)


def copies_kernel(x_ref, o_ref, sem):
    count = o_ref.shape[0]
    copies = [pltpu.make_async_copy(x_ref, o_ref.at[i], sem.at[i]) for i in range(count)]
    for copy in copies:
        copy.start()
    for copy in copies:
        copy.wait()


def copies_of(x, count):
    return pl.pallas_call(
        copies_kernel,
        out_shape=like((count,) + x.shape, x.dtype),
        in_specs=[VMEM],
        out_specs=ANY,
        scratch_shapes=[pltpu.SemaphoreType.DMA((count,))],
        compiler_params=params(4),
        cost_estimate=cost(0, x.size * 2 * (count + 1)),
    )(x)


def sum_copies_kernel(x_ref, o_ref):
    total = x_ref[0].astype(F32)
    for i in range(1, x_ref.shape[0]):
        total = total + x_ref[i].astype(F32)
    total = total.astype(o_ref.dtype)
    for i in range(o_ref.shape[0]):
        o_ref[i] = total


def sum_copies(x, count):
    return pl.pallas_call(
        sum_copies_kernel,
        out_shape=like((count,) + x.shape[1:]),
        in_specs=[VMEM],
        out_specs=VMEM,
        compiler_params=params(4),
        cost_estimate=cost(x.size, x.size * 2),
    )(x)


def partial_kernel(me_ref, tokens_ref, weight_ref, *outs):
    count = len(outs)
    groups = 3
    rows = tokens_ref.shape[0] // (count * groups)
    scaled = (weight_ref[...] * FACTOR).astype(BF16)
    for shift, out in enumerate(outs):
        at = lax.rem(me_ref[0] + shift, count)
        block = jnp.concatenate(
            [tokens_ref[pl.ds(pl.multiple_of((g * count + at) * rows, rows), rows), :] for g in range(groups)], 0
        )
        out[...] = jnp.dot(block, scaled, preferred_element_type=F32).astype(out.dtype)


def partial_keys(tokens, weight, count):
    rows, width = tokens.shape[0] // count, weight.shape[1]
    return pl.pallas_call(
        partial_kernel,
        out_shape=[like((rows, width))] * count,
        in_specs=[SMEM, VMEM, VMEM],
        out_specs=[VMEM] * count,
        compiler_params=params(16),
        cost_estimate=cost(2 * tokens.size * width, 4 << 20),
    )(lax.axis_index("x").reshape(1), tokens, weight)


def hold_kernel(*refs):
    pass


def hold_until(xs, dep):
    count = len(xs)
    return pl.pallas_call(
        hold_kernel,
        out_shape=[like(x.shape, x.dtype) for x in xs],
        in_specs=[ANY] * (count + 1),
        out_specs=[ANY] * count,
        input_output_aliases={i: i for i in range(count)},
        cost_estimate=cost(0, 0),
        compiler_params=params(1),
    )(*xs, dep)


def ring_sum_kernel(me_ref, *refs):
    parts, outs = refs[:-3], refs[-3:]
    count = len(outs)
    rows = outs[0].shape[0]
    for shift, out in enumerate(outs):
        at = pl.ds(pl.multiple_of(lax.rem(me_ref[0] + shift, count) * rows, rows), rows)
        total = parts[0][at, :].astype(F32)
        for part in parts[1:]:
            total = total + part[at, :].astype(F32)
        out[...] = total.astype(out.dtype)


def ring_sum(parts):
    rows, width = parts[0].shape
    return pl.pallas_call(
        ring_sum_kernel,
        out_shape=[like((rows // 3, width), F32)] + [like((rows // 3, width))] * 2,
        in_specs=[SMEM] + [VMEM] * len(parts),
        out_specs=[VMEM] * 3,
        compiler_params=params(8),
        cost_estimate=cost(4 * rows * width, 4 << 20),
    )(lax.axis_index("zl").reshape(1), *parts)


def send(x, axis, shift):
    count = lax.axis_size(axis)
    return lax.ppermute(x, axis, [(i, (i + shift) % count) for i in range(count)])


def back_kernel(piece_ref, weight_ref, o_ref, scaled_ref):
    @pl.when(pl.program_id(0) == 0)
    def _():
        scaled_ref[...] = (weight_ref[...] * FACTOR).astype(BF16)

    o_ref[...] = lax.dot_general(
        piece_ref[...], scaled_ref[...], (((1,), (1,)), ((), ())), preferred_element_type=F32
    ).astype(o_ref.dtype)


def token_gradient(piece, weight):
    rows, width = piece.shape
    feats = weight.shape[0]
    tile = 256
    return pl.pallas_call(
        back_kernel,
        out_shape=like((rows, feats)),
        grid=(rows // tile,),
        in_specs=[pl.BlockSpec((tile, width), lambda i: (i, 0)), pl.BlockSpec((feats, width), lambda i: (0, 0))],
        out_specs=pl.BlockSpec((tile, feats), lambda i: (i, 0)),
        scratch_shapes=[pltpu.VMEM((feats, width), BF16)],
        compiler_params=params(16),
        cost_estimate=cost(2 * rows * width * feats, 4 << 20),
    )(piece, weight)


def local(tokens, key_grad, weight, moment, second):
    rows, width, feats = tokens.shape[0], key_grad.shape[1], tokens.shape[1]
    size = lax.axis_size
    piece = swap_parts(copies_of(key_grad, size("zl") * size("x")), BLK).reshape(rows, width)
    own, *out = partial_keys(tokens, weight, size("x"))

    grad = lax.dot_general(tokens, piece, (((0,), (0,)), ((), ())), preferred_element_type=F32) * FACTOR
    grad = grad.astype(BF16)
    pair = size("y") * size("c")
    shares = swap_parts(grad.reshape(pair, feats // pair, width), PAIR)
    shares = swap_parts(sum_copies(shares, size("zh")), "zh")
    half = swap_parts(sum_copies(shares, size("y")), "y").reshape(feats // size("c"), width)
    weight_grad = lax.all_gather(half, "c", axis=0, tiled=True).astype(F32)

    out = hold_until(out, grad)
    got = [send(x, "x", 1 + i) for i, x in enumerate(out)]
    mine, *out = ring_sum([own] + got)
    got = [send(x, "zl", 1 + i) for i, x in enumerate(out)]
    keys = (mine + got[0].astype(F32) + got[1].astype(F32)).astype(BF16)

    back = token_gradient(piece, weight)
    weight_new, moment_new, second_new = optimize(weight, moment, second, weight_grad)
    return (keys, back, weight_grad, weight_new, moment_new, second_new)


def solution(mesh):
    fine = Mesh(mesh.devices.reshape(8, 4, 2, 3, 4), AXES)
    in_specs = (P(DP, BLK), P(DP + BLK, None), P(BLK, None), P(BLK, None), P(BLK, None))
    out_specs = (P(DP + BLK, None), P(DP, BLK), P(BLK, None), P(BLK, None), P(BLK, None), P(BLK, None))
    return jax.shard_map(local, mesh=fine, in_specs=in_specs, out_specs=out_specs, check_vma=False)
```

time: 730 us -> 115 us (0.16)
  waiting for transfers between devices: 618 us -> 3.27 us
  starting transfers between devices: 0.08 us -> 35.8 us
  blocking collectives: 74.8 us -> 56.5 us
  between operations: 14.1 us -> 0.74 us
  Pallas kernels: 0 us -> 9.65 us
  matrix products: 10.9 us -> 1.8 us
    psum x1 -> x0, waiting for transfers between devices: 554 us -> none  [local(): weight_grad = lax.psum(local_grad, 'dp')]
    psum x1 -> x0, blocking collectives: 74.8 us -> none  [local(): summed = lax.psum(partial_value, 'blk')]
    all_gather x1 -> x0, waiting for transfers between devices: 63.6 us -> none  [local(): piece = lax.all_gather(key_grad, 'blk', axis=0, tiled=True)]
    all_to_all x0 -> x2, blocking collectives: none -> 52.9 us  [swap_parts(): return lax.all_to_all(x, axes, 0, 0, tiled=True)]
    all_to_all x0 -> x2, starting transfers between devices: none -> 20.2 us  [swap_parts(): return lax.all_to_all(x, axes, 0, 0, tiled=True)]
    ppermute x0 -> x5, starting transfers between devices: none -> 15.7 us  [send(): lax.ppermute(x, axis, [(i, (i + shift) % count) for i in range(count)])]
    pallas_call x0 -> x7, Pallas kernels: none -> 9.65 us  [the longest x1 3.57 us: token_gradient(): pl.pallas_call(back_kernel, out_shape=like((rows, feats)), grid=(rows //...]
    dot_general x2 -> x0, matrix products: 7.5 us -> none  [the longest x1 3.9 us: local(): partial_value = jnp.dot(tokens, scaled, preferred_element_type=jnp.float32)]
  transfers between devices with their start and end apart: 2 -> 7, of which waited for: 2 -> 2; matrix products, arithmetic and copies ran while one was open for 2% -> 1% of each run, Pallas kernels for 0% -> 7%
where the time goes in v1:
time: 115 us; the launch traced here: 114 us
  blocking collectives  56.5 us (49%)
  starting transfers between devices  35.8 us (31%)
  Pallas kernels  9.65 us (8%)
  other arithmetic  4.3 us (4%)
  waiting for transfers between devices  3.27 us (3%)
  local copies, waits for them, and re-layouts  2.31 us (2%)
  matrix products  1.8 us (2%)
    all_to_all x2, blocking collectives, swap_parts(): return lax.all_to_all(x, axes, 0, 0, tiled=True)  52.9 us
    all_to_all x2, starting transfers between devices, swap_parts(): return lax.all_to_all(x, axes, 0, 0, tiled=True)  20.2 us
    ppermute x5, starting transfers between devices, send(): lax.ppermute(x, axis, [(i, (i + shift) % count) for i in range(count)])  15.7 us
    sub x1, other arithmetic, optimize(): weight_new = weight - 0.05 * (step_dir + 0.1 * weight)  3.6 us
    pallas_call x1, Pallas kernels, token_gradient(): pl.pallas_call(back_kernel, out_shape=like((rows, feats)), grid=(rows //...  3.57 us
    all_gather x1, blocking collectives, local(): weight_grad = lax.all_gather(half, 'c', axis=0, tiled=True).astype(F32)  3.56 us
    unnamed x10, local copies, waits for them, and re-layouts  2.31 us
  transfers between devices with their start and end apart: 7, of which 2 were waited for; matrix products, arithmetic and copies ran while one was open for 1% of the time, Pallas kernels for 7%

profile of v1, /device:TPU:1, one launch (start us, length us, event | category | flops | bytes accessed | tf_op | source)
XLA Modules:
  0.0 114.4 jit_solution(3281919900641636975)
XLA Ops:
  0.6 0.9 copy-done.3
  1.5 2.1 %shard_map.101 = bf16[12,128,512]{2,1,0:T(8,128)(2,1)S(1)} custom-call(bf16[128,512]{1,0:T(8,128)(2,1)S(1)} %copy-done.3), custom_call_target="tpu_custom_call" | custom-call | bytes 1703936 | tf_op jit(solution)/shard_map/pallas_call | solution.py:57
  3.7 0.0 copy-start.1
  3.7 29.0 %all_to_all.20 = bf16[12,128,512]{2,1,0:T(8,128)(2,1)S(1)} all-to-all(bf16[12,128,512]{2,1,0:T(8,128)(2,1)S(1)} %shard_map.101), channel_id=1, replica_groups=mesh['y'=8,'zh'=4,'c'=2,'zl'=3,'x'=4] {'zl','x'}, dimensions={0} | all-to-all | bytes 3145728 | tf_op jit(solution)/shard_map/all_to_all | solution.py:44
  32.7 0.0 copy-done.1
  32.7 1.8 %fusion.refs_3_ = bf16[512,512]{1,0:T(8,128)(2,1)} fusion(bf16[1536,512]{1,0:T(8,128)(2,1)S(1)} %copy-done.1, bf16[1536,512]{1,0:T(8,128)(2,1)S(1)} %bitcast.7), kind=kOutput, calls=%fused_computation.2 | convolution fusion | flops 805830656 | bytes 3670016 | tf_op jit(solution)/shard_map/dot_general | solution.py:191
  34.5 14.2 %all-to-all-start.1 = ((bf16[16,32,512]{2,1,0:T(8,128)(2,1)}), bf16[16,32,512]{2,1,0:T(8,128)(2,1)S(1)}, u32[]{:S(2)}, u32[]{:S(2)}) async-start(bf16[16,32,512]{2,1,0:T(8,128)(2,1)} %bitcast.3), calls=%async_computation.1 | async-start | bytes 1048576 | tf_op jit(solution)/shard_map/all_to_all | solution.py:44
  48.7 0.0 copy-done
  48.7 0.0 copy-start.2
  48.7 1.4 %copy-done.2 = bf16[1536,512]{1,0:T(8,128)(2,1)S(1)} copy-done((bf16[1536,512]{1,0:T(8,128)(2,1)S(1)}, bf16[1536,512]{1,0:T(8,128)(2,1)}, u32[]{:S(2)}) %copy-start.2) | copy-done | bytes 1572888
  50.1 1.7 %shard_map.100 = (bf16[384,512]{1,0:T(8,128)(2,1)S(1)}, bf16[384,512]{1,0:T(8,128)(2,1)}, bf16[384,512]{1,0:T(8,128)(2,1)}, bf16[384,512]{1,0:T(8,128)(2,1)}) custom-call(s32[1]{0:T(128)} %bitcast.1.me_ref, bf16[1536,512]{1,0:T(8,128)(2,1)S(1)} %copy-done.2, f32[512,512]{1,0:T(8,128)S(1)} %copy-done), custom_call_target="tpu_custom_call" | custom-call | flops 805306368 | bytes 4194304 | tf_op jit(solution)/shard_map/pallas_call | solution.py:103
  51.8 2.4 %collective-permute-start = (bf16[384,512]{1,0:T(8,128)(2,1)}, bf16[384,512]{1,0:T(8,128)(2,1)}, u32[]{:S(2)}, u32[]{:S(2)}) collective-permute-start(bf16[384,512]{1,0:T(8,128)(2,1)} %get-tuple-element.20), channel_id=1, source_target_pairs={{0,1},{1,2},{2,3},{3,0},{4,5},{5,6},{6,7},{7,4},{8,9},{9,10},{10,1... | collective-permute-start | bytes 1179656 | tf_op jit(solution)/shard_map/ppermute | solution.py:156
  54.2 4.9 %collective-permute-start.1 = (bf16[384,512]{1,0:T(8,128)(2,1)}, bf16[384,512]{1,0:T(8,128)(2,1)}, u32[]{:S(2)}, u32[]{:S(2)}) collective-permute-start(bf16[384,512]{1,0:T(8,128)(2,1)} %get-tuple-element.21), channel_id=1, source_target_pairs={{0,2},{1,3},{2,0},{3,1},{4,6},{5,7},{6,4},{7,5},{8,10},{9,11},{10,... | collective-permute-start | bytes 1179656 | tf_op jit(solution)/shard_map/ppermute | solution.py:156
  59.1 2.2 %collective-permute-start.2 = (bf16[384,512]{1,0:T(8,128)(2,1)}, bf16[384,512]{1,0:T(8,128)(2,1)}, u32[]{:S(2)}, u32[]{:S(2)}) collective-permute-start(bf16[384,512]{1,0:T(8,128)(2,1)} %get-tuple-element.22), channel_id=1, source_target_pairs={{0,3},{1,0},{2,1},{3,2},{4,7},{5,4},{6,5},{7,6},{8,11},{9,8},{10,9... | collective-permute-start | bytes 1179656 | tf_op jit(solution)/shard_map/ppermute | solution.py:156
  61.4 2.1 %all-to-all-done.1.x_ref = bf16[16,32,512]{2,1,0:T(8,128)(2,1)S(1)} async-done(((bf16[16,32,512]{2,1,0:T(8,128)(2,1)}), bf16[16,32,512]{2,1,0:T(8,128)(2,1)S(1)}, u32[]{:S(2)}, u32[]{:S(2)}) %all-to-all-start.1) | async-done | bytes 524320 | tf_op jit(solution)/shard_map/all_to_all | solution.py:44
  63.4 0.1 shard_map.105
  63.5 23.9 %all_to_all.21.x_ref = bf16[4,32,512]{2,1,0:T(8,128)(2,1)S(1)} all-to-all(bf16[4,32,512]{2,1,0:T(8,128)(2,1)S(1)} %shard_map.105), channel_id=1, replica_groups=mesh['y'=8,'zh'=4,'c'=2,'zl'=3,'x'=4] {'zh'}, dimensions={0} | all-to-all | bytes 262144 | tf_op jit(solution)/shard_map/all_to_all | solution.py:44
  87.4 0.7 shard_map.106
  88.2 6.0 %all-to-all-start.3 = ((bf16[8,32,512]{2,1,0:T(8,128)(2,1)}), bf16[8,32,512]{2,1,0:T(8,128)(2,1)S(1)}, u32[]{:S(2)}, u32[]{:S(2)}) async-start(bf16[8,32,512]{2,1,0:T(8,128)(2,1)} %shard_map.106), calls=%async_computation.3 | async-start | bytes 524288 | tf_op jit(solution)/shard_map/all_to_all | solution.py:44
  94.1 0.0 collective-permute-done.refs_1_
  94.1 0.0 collective-permute-done.1.refs_2_
  94.1 0.0 collective-permute-done.2.refs_3_
  94.1 1.4 %shard_map.103 = (f32[128,512]{1,0:T(8,128)S(1)}, bf16[128,512]{1,0:T(8,128)(2,1)S(1)}, bf16[128,512]{1,0:T(8,128)(2,1)S(1)}) custom-call(s32[1]{0:T(128)} %bitcast.me_ref, bf16[384,512]{1,0:T(8,128)(2,1)S(1)} %get-tuple-element.16.refs_0_, bf16[384,512]{1,0:T(8,128)(2,1)} %collective-permute-done.refs_1_, bf16[384,512]{1,0:T(8,128)(2,1)} %collective-permute-done.1.refs_2_, ...), custom_call_target="tpu_custom_call" | custom-call | flops 786432 | bytes 4194304 | tf_op jit(solution)/shard_map/pallas_call | solution.py:144
  95.6 4.1 %collective-permute-start.3 = (bf16[128,512]{1,0:T(8,128)(2,1)S(1)}, bf16[128,512]{1,0:T(8,128)(2,1)S(1)}, u32[]{:S(2)}, u32[]{:S(2)}) collective-permute-start(bf16[128,512]{1,0:T(8,128)(2,1)S(1)} %get-tuple-element.24), channel_id=1, source_target_pairs={{0,4},{4,8},{8,0},{1,5},{5,9},{9,1},{2,6},{6,10},{10,2},{3,7},{7,1... | collective-permute-start | bytes 393224 | tf_op jit(solution)/shard_map/ppermute | solution.py:156
  99.6 2.1 %collective-permute-start.4 = (bf16[128,512]{1,0:T(8,128)(2,1)S(1)}, bf16[128,512]{1,0:T(8,128)(2,1)S(1)}, u32[]{:S(2)}, u32[]{:S(2)}) collective-permute-start(bf16[128,512]{1,0:T(8,128)(2,1)S(1)} %get-tuple-element.25), channel_id=1, source_target_pairs={{0,8},{4,0},{8,4},{1,9},{5,1},{9,5},{2,10},{6,2},{10,6},{3,11},{7,... | collective-permute-start | bytes 393224 | tf_op jit(solution)/shard_map/ppermute | solution.py:156
  101.8 3.6 %shard_map.104 = bf16[1536,512]{1,0:T(8,128)(2,1)} custom-call(bf16[1536,512]{1,0:T(8,128)(2,1)S(1)} %bitcast.8, f32[512,512]{1,0:T(8,128)S(1)} %copy-done), custom_call_target="tpu_custom_call" | custom-call | flops 805306368 | bytes 4194304 | tf_op jit(solution)/shard_map/pallas_call | solution.py:173
  105.3 0.0 collective-permute-done.3
  105.3 1.2 %collective-permute-done.4 = bf16[128,512]{1,0:T(8,128)(2,1)S(1)} collective-permute-done((bf16[128,512]{1,0:T(8,128)(2,1)S(1)}, bf16[128,512]{1,0:T(8,128)(2,1)S(1)}, u32[]{:S(2)}, u32[]{:S(2)}) %collective-permute-start.4) | collective-permute-done | bytes 131104 | tf_op jit(solution)/shard_map/ppermute | solution.py:156
  106.5 0.7 add_convert_fusion
  107.2 0.0 all-to-all-done.3
  107.2 3.6 %all_gather.3 = bf16[512,512]{1,0:T(8,128)(2,1)S(1)} all-gather(bf16[256,512]{1,0:T(8,128)(2,1)S(1)} %bitcast.9), channel_id=1, replica_groups=mesh['y'=8,'zh'=4,'c'=2,'zl'=3,'x'=4] {'c'}, dimensions={0}, use_global_device_ids=true | all-gather | bytes 786432 | tf_op jit(solution)/shard_map/all_gather | solution.py:197
  110.8 3.6 %multiply_subtract_fusion = (f32[512,512]{1,0:T(8,128)}, f32[512,512]{1,0:T(8,128)}, f32[512,512]{1,0:T(8,128)}, f32[512,512]{1,0:T(8,128)}) fusion(f32[512,512]{1,0:T(8,128)S(1)} %copy-done, f32[512,512]{1,0:T(8,128)S(1)} %copy-done.4, f32[512,512]{1,0:T(8,128)} %param.9, bf16[512,512]{1,0:T(8,128)(2,1)S(1)} %all_gather.3), kind=kLoop, calls=%fused_computation.4 | loop fusion | flops 4194304 | bytes 7864320 | tf_op jit(solution)/shard_map/sub | solution.py:27
  (5 shorter events, 0.0 us)
Async XLA Ops:
  0.6 0.9 copy-start.3
  3.7 29.0 %copy-start.1 = (bf16[1536,512]{1,0:T(8,128)(2,1)S(1)}, bf16[1536,512]{1,0:T(8,128)(2,1)}, u32[]{:S(2)}) copy-start(bf16[1536,512]{1,0:T(8,128)(2,1)} %tokens_ref.1) | copy-start | bytes 4718596
  32.7 16.0 %copy-start = (f32[512,512]{1,0:T(8,128)S(1)}, f32[512,512]{1,0:T(8,128)}, u32[]{:S(2)}) copy-start(f32[512,512]{1,0:T(8,128)} %weight_ref.3) | copy-start | bytes 3145732
  34.5 29.0 %all-to-all-start.1 = ((bf16[16,32,512]{2,1,0:T(8,128)(2,1)}), bf16[16,32,512]{2,1,0:T(8,128)(2,1)S(1)}, u32[]{:S(2)}, u32[]{:S(2)}) async-start(bf16[16,32,512]{2,1,0:T(8,128)(2,1)} %bitcast.3), calls=%async_computation.1 | async-start | bytes 1048576 | tf_op jit(solution)/shard_map/all_to_all | solution.py:44
  48.7 1.4 %copy-start.2 = (bf16[1536,512]{1,0:T(8,128)(2,1)S(1)}, bf16[1536,512]{1,0:T(8,128)(2,1)}, u32[]{:S(2)}) copy-start(bf16[1536,512]{1,0:T(8,128)(2,1)} %tokens_ref.1) | copy-start | bytes 4718596
  51.8 42.3 %collective-permute-start = (bf16[384,512]{1,0:T(8,128)(2,1)}, bf16[384,512]{1,0:T(8,128)(2,1)}, u32[]{:S(2)}, u32[]{:S(2)}) collective-permute-start(bf16[384,512]{1,0:T(8,128)(2,1)} %get-tuple-element.20), channel_id=1, source_target_pairs={{0,1},{1,2},{2,3},{3,0},{4,5},{5,6},{6,7},{7,4},{8,9},{9,10},{10,1... | collective-permute-start | bytes 1179656 | tf_op jit(solution)/shard_map/ppermute | solution.py:156
  54.2 39.9 %collective-permute-start.1 = (bf16[384,512]{1,0:T(8,128)(2,1)}, bf16[384,512]{1,0:T(8,128)(2,1)}, u32[]{:S(2)}, u32[]{:S(2)}) collective-permute-start(bf16[384,512]{1,0:T(8,128)(2,1)} %get-tuple-element.21), channel_id=1, source_target_pairs={{0,2},{1,3},{2,0},{3,1},{4,6},{5,7},{6,4},{7,5},{8,10},{9,11},{10,... | collective-permute-start | bytes 1179656 | tf_op jit(solution)/shard_map/ppermute | solution.py:156
  59.1 35.0 %collective-permute-start.2 = (bf16[384,512]{1,0:T(8,128)(2,1)}, bf16[384,512]{1,0:T(8,128)(2,1)}, u32[]{:S(2)}, u32[]{:S(2)}) collective-permute-start(bf16[384,512]{1,0:T(8,128)(2,1)} %get-tuple-element.22), channel_id=1, source_target_pairs={{0,3},{1,0},{2,1},{3,2},{4,7},{5,4},{6,5},{7,6},{8,11},{9,8},{10,9... | collective-permute-start | bytes 1179656 | tf_op jit(solution)/shard_map/ppermute | solution.py:156
  88.2 19.1 %all-to-all-start.3 = ((bf16[8,32,512]{2,1,0:T(8,128)(2,1)}), bf16[8,32,512]{2,1,0:T(8,128)(2,1)S(1)}, u32[]{:S(2)}, u32[]{:S(2)}) async-start(bf16[8,32,512]{2,1,0:T(8,128)(2,1)} %shard_map.106), calls=%async_computation.3 | async-start | bytes 524288 | tf_op jit(solution)/shard_map/all_to_all | solution.py:44
  95.6 9.8 %collective-permute-start.3 = (bf16[128,512]{1,0:T(8,128)(2,1)S(1)}, bf16[128,512]{1,0:T(8,128)(2,1)S(1)}, u32[]{:S(2)}, u32[]{:S(2)}) collective-permute-start(bf16[128,512]{1,0:T(8,128)(2,1)S(1)} %get-tuple-element.24), channel_id=1, source_target_pairs={{0,4},{4,8},{8,0},{1,5},{5,9},{9,1},{2,6},{6,10},{10,2},{3,7},{7,1... | collective-permute-start | bytes 393224 | tf_op jit(solution)/shard_map/ppermute | solution.py:156
  99.6 6.9 %collective-permute-start.4 = (bf16[128,512]{1,0:T(8,128)(2,1)S(1)}, bf16[128,512]{1,0:T(8,128)(2,1)S(1)}, u32[]{:S(2)}, u32[]{:S(2)}) collective-permute-start(bf16[128,512]{1,0:T(8,128)(2,1)S(1)} %get-tuple-element.25), channel_id=1, source_target_pairs={{0,8},{4,0},{8,4},{1,9},{5,1},{9,5},{2,10},{6,2},{10,6},{3,11},{7,... | collective-permute-start | bytes 393224 | tf_op jit(solution)/shard_map/ppermute | solution.py:156
  105.3 5.4 %copy-start.4 = (f32[512,512]{1,0:T(8,128)S(1)}, f32[512,512]{1,0:T(8,128)}, u32[]{:S(2)}) copy-start(f32[512,512]{1,0:T(8,128)} %param.8) | copy-start | bytes 3145732

commit v2 on v1

v2 whole, which is shorter than its diff:
```python
import jax
import jax.numpy as jnp
from jax import lax
from jax.experimental import pallas as pl
from jax.experimental.pallas import tpu as pltpu
from jax.sharding import Mesh, PartitionSpec as P

D = 6144
STEP = 100
FACTOR = D ** (-0.5)
AXES = ("y", "zh", "c", "zl", "x")
DP = ("y", "zh", "c")
BLK = ("zl", "x")
PAIR = ("c", "y")
BRIEF = pl.CostEstimate(flops=1, bytes_accessed=1, transcendentals=0)
BF16, F32 = jnp.bfloat16, jnp.float32
VMEM = pl.BlockSpec(memory_space=pltpu.VMEM)
SMEM = pl.BlockSpec(memory_space=pltpu.SMEM)
ANY = pl.BlockSpec(memory_space=pl.ANY)


def optimize(weight, moment, second, weight_grad):
    moment_new = 0.9 * moment + 0.1 * weight_grad
    second_new = 0.999 * second + 0.001 * weight_grad * weight_grad
    first_fix = 1.0 / (1.0 - 0.9**STEP)
    second_fix = 1.0 / (1.0 - 0.999**STEP)
    step_dir = moment_new * first_fix / (jnp.sqrt(second_new * second_fix) + 1e-08)
    weight_new = weight - 0.05 * (step_dir + 0.1 * weight)
    return (weight_new, moment_new, second_new)


def params(mib):
    return pltpu.CompilerParams(vmem_limit_bytes=mib << 20)


def like(shape, dtype=BF16):
    return jax.ShapeDtypeStruct(shape, dtype)


TOKEN = like((8, 128), F32)


def swap_parts(x, axes):
    return lax.all_to_all(x, axes, 0, 0, tiled=True)


def copies_kernel(x_ref, o_ref):
    for i in range(o_ref.shape[0]):
        o_ref[i] = x_ref[...]


def copies_of(x, count):
    return pl.pallas_call(
        copies_kernel,
        out_shape=like((count,) + x.shape, x.dtype),
        in_specs=[VMEM],
        out_specs=VMEM,
        compiler_params=params(4),
        cost_estimate=BRIEF,
    )(x)


def sum_copies_kernel(x_ref, *refs):
    o_ref, token_ref = refs[-2:]
    total = x_ref[0].astype(F32)
    for i in range(1, x_ref.shape[0]):
        total = total + x_ref[i].astype(F32)
    total = total.astype(o_ref.dtype)
    for i in range(o_ref.shape[0]):
        o_ref[i] = total
    token_ref[...] = jnp.zeros(token_ref.shape, F32)


def sum_copies(x, count, *tokens):
    return pl.pallas_call(
        sum_copies_kernel,
        out_shape=[like((count,) + x.shape[1:]), TOKEN],
        in_specs=[VMEM] + [ANY] * len(tokens),
        out_specs=[VMEM] * 2,
        compiler_params=params(4),
        cost_estimate=BRIEF,
    )(x, *tokens)


def partial_kernel(me_ref, tokens_ref, weight_ref, dep_ref, *outs):
    count = len(outs)
    groups = 3
    rows = tokens_ref.shape[0] // (count * groups)
    scaled = (weight_ref[...] * FACTOR).astype(BF16)
    for shift, out in enumerate(outs):
        at = lax.rem(me_ref[0] + shift, count)
        block = jnp.concatenate(
            [tokens_ref[pl.ds(pl.multiple_of((g * count + at) * rows, rows), rows), :] for g in range(groups)], 0
        )
        out[...] = jnp.dot(block, scaled, preferred_element_type=F32).astype(out.dtype)


def partial_keys(tokens, weight, count, dep):
    rows, width = tokens.shape[0] // count, weight.shape[1]
    return pl.pallas_call(
        partial_kernel,
        out_shape=[like((rows, width))] * count,
        in_specs=[SMEM, VMEM, VMEM, ANY],
        out_specs=[VMEM] * count,
        compiler_params=params(16),
        cost_estimate=BRIEF,
    )(lax.axis_index("x").reshape(1), tokens, weight, dep)


def ring_sum_kernel(me_ref, after_ref, *refs):
    parts, outs, token_ref = refs[:-4], refs[-4:-1], refs[-1]
    token_ref[...] = jnp.zeros(token_ref.shape, F32)
    count = len(outs)
    rows = outs[0].shape[0]
    for shift, out in enumerate(outs):
        at = pl.ds(pl.multiple_of(lax.rem(me_ref[0] + shift, count) * rows, rows), rows)
        total = parts[0][at, :].astype(F32)
        for part in parts[1:]:
            total = total + part[at, :].astype(F32)
        out[...] = total.astype(out.dtype)


def ring_sum(parts, token):
    rows, width = parts[0].shape
    return pl.pallas_call(
        ring_sum_kernel,
        out_shape=[like((rows // 3, width), F32)] + [like((rows // 3, width))] * 2 + [TOKEN],
        in_specs=[SMEM, ANY] + [VMEM] * len(parts),
        out_specs=[VMEM] * 4,
        compiler_params=params(8),
        cost_estimate=BRIEF,
    )(lax.axis_index("zl").reshape(1), token, *parts)


def finish_kernel(g_ref, weight_ref, moment_ref, second_ref, a_ref, b_ref, c_ref, *outs):
    grad = g_ref[...].astype(F32)
    new = optimize(weight_ref[...], moment_ref[...], second_ref[...], grad)
    keys = (a_ref[...] + b_ref[...].astype(F32) + c_ref[...].astype(F32)).astype(BF16)
    for out, value in zip(outs, (keys, grad) + new, strict=True):
        out[...] = value


def finish(grad, weight, moment, second, parts):
    (rows, width), (few, _) = grad.shape, parts[0].shape
    steps = 4
    big = pl.BlockSpec((rows // steps, width), lambda i: (i, 0))
    small = pl.BlockSpec((few // steps, width), lambda i: (i, 0))
    return pl.pallas_call(
        finish_kernel,
        out_shape=[like((few, width))] + [like((rows, width), F32)] * 4,
        grid=(steps,),
        in_specs=[big] * 4 + [small] * 3,
        out_specs=[small] + [big] * 4,
        compiler_params=params(16),
        cost_estimate=BRIEF,
    )(grad, weight, moment, second, *parts)


def send(x, axis, shift):
    count = lax.axis_size(axis)
    return lax.ppermute(x, axis, [(i, (i + shift) % count) for i in range(count)])


def back_kernel(after_ref, piece_ref, weight_ref, o_ref, token_ref, scaled_ref):
    @pl.when(pl.program_id(0) == 0)
    def _():
        scaled_ref[...] = (weight_ref[...] * FACTOR).astype(BF16)
        token_ref[...] = jnp.zeros(token_ref.shape, F32)

    o_ref[...] = lax.dot_general(
        piece_ref[...], scaled_ref[...], (((1,), (1,)), ((), ())), preferred_element_type=F32
    ).astype(o_ref.dtype)


def token_gradient(piece, weight, token):
    rows, width = piece.shape
    feats = weight.shape[0]
    tile = 512
    return pl.pallas_call(
        back_kernel,
        out_shape=[like((rows, feats)), TOKEN],
        grid=(rows // tile,),
        in_specs=[
            ANY,
            pl.BlockSpec((tile, width), lambda i: (i, 0)),
            pl.BlockSpec((feats, width), lambda i: (0, 0)),
        ],
        out_specs=[pl.BlockSpec((tile, feats), lambda i: (i, 0)), pl.BlockSpec((8, 128), lambda i: (0, 0))],
        scratch_shapes=[pltpu.VMEM((feats, width), BF16)],
        compiler_params=params(16),
        cost_estimate=BRIEF,
    )(token, piece, weight)


def local(tokens, key_grad, weight, moment, second):
    rows, width, feats = tokens.shape[0], key_grad.shape[1], tokens.shape[1]
    size = lax.axis_size
    piece = swap_parts(copies_of(key_grad, size("zl") * size("x")), BLK).reshape(rows, width)

    grad = lax.dot_general(tokens, piece, (((0,), (0,)), ((), ())), preferred_element_type=F32) * FACTOR
    grad = grad.astype(BF16)
    own, *out = partial_keys(tokens, weight, size("x"), grad)
    got = [send(x, "x", 1 + i) for i, x in enumerate(out)]
    pair = size("y") * size("c")
    shares, first = sum_copies(swap_parts(grad.reshape(pair, feats // pair, width), PAIR), size("zh"))
    back, after_back = token_gradient(piece, weight, first)
    mine, *out, after_keys = ring_sum([own] + got, first)
    got = [send(x, "zl", 1 + i) for i, x in enumerate(out)]
    shares, _ = sum_copies(swap_parts(shares, "zh"), size("y"), after_back, after_keys)
    half = swap_parts(shares, "y").reshape(feats // size("c"), width)
    full = lax.all_gather(half, "c", axis=0, tiled=True)
    keys, weight_grad, *new = finish(full, weight, moment, second, [mine] + got)
    return (keys, back, weight_grad, *new)


def solution(mesh):
    fine = Mesh(mesh.devices.reshape(8, 4, 2, 3, 4), AXES)
    in_specs = (P(DP, BLK), P(DP + BLK, None), P(BLK, None), P(BLK, None), P(BLK, None))
    out_specs = (P(DP + BLK, None), P(DP, BLK), P(BLK, None), P(BLK, None), P(BLK, None), P(BLK, None))
    return jax.shard_map(local, mesh=fine, in_specs=in_specs, out_specs=out_specs, check_vma=False)
```

time: 115 us -> 112 us (0.974)
  blocking collectives: 56.5 us -> 34.4 us
  starting transfers between devices: 35.8 us -> 50.1 us
  waiting for transfers between devices: 3.27 us -> 10.8 us
  other arithmetic: 4.3 us -> 0 us
  local copies, waits for them, and re-layouts: 2.31 us -> 4.18 us
    all_to_all x2 -> x1, blocking collectives: 52.9 us -> 29 us  [swap_parts(): return lax.all_to_all(x, axes, 0, 0, tiled=True)]
    all_to_all x2 -> x3, starting transfers between devices: 20.2 us -> 34.4 us  [swap_parts(): return lax.all_to_all(x, axes, 0, 0, tiled=True)]
    all_to_all x2 -> x3, waiting for transfers between devices: 2.09 us -> 10.8 us  [swap_parts(): return lax.all_to_all(x, axes, 0, 0, tiled=True)]
    sub x1 -> x0, other arithmetic: 3.6 us -> none  [optimize(): weight_new = weight - 0.05 * (step_dir + 0.1 * weight)]
    pallas_call x1, Pallas kernels: 2.12 us -> 0.1 us  [copies_of(): pl.pallas_call(copies_kernel, out_shape=like((count,) + x.shape, x.dtype)...]
    all_gather x1, blocking collectives: 3.56 us -> 5.44 us  [local(): full = lax.all_gather(half, 'c', axis=0, tiled=True)]
    unnamed x10 -> x14, local copies, waits for them, and re-layouts: 2.31 us -> 4.18 us
    pallas_call x4, Pallas kernels: 4.37 us -> 5.97 us  [the longest x1 2.61 us: token_gradient(): pl.pallas_call(back_kernel, out_shape=[like((rows, feats)), TOKEN], grid=...]
  transfers between devices with their start and end apart: 7 -> 8, of which waited for: 2 -> 3; matrix products, arithmetic and copies ran while one was open for 1% -> 0% of each run, Pallas kernels for 7% -> 5%
where the time goes in v2:
time: 112 us; the launch traced here: 111 us
  starting transfers between devices  50.1 us (45%)
  blocking collectives  34.4 us (31%)
  waiting for transfers between devices  10.8 us (10%)
  Pallas kernels  9.32 us (8%)
  local copies, waits for them, and re-layouts  4.18 us (4%)
  matrix products  1.8 us (2%)
    all_to_all x3, starting transfers between devices, swap_parts(): return lax.all_to_all(x, axes, 0, 0, tiled=True)  34.4 us
    all_to_all x1, blocking collectives, swap_parts(): return lax.all_to_all(x, axes, 0, 0, tiled=True)  29 us
    ppermute x5, starting transfers between devices, send(): lax.ppermute(x, axis, [(i, (i + shift) % count) for i in range(count)])  15.7 us
    all_to_all x3, waiting for transfers between devices, swap_parts(): return lax.all_to_all(x, axes, 0, 0, tiled=True)  10.8 us
    all_gather x1, blocking collectives, local(): full = lax.all_gather(half, 'c', axis=0, tiled=True)  5.44 us
    unnamed x14, local copies, waits for them, and re-layouts  4.18 us
    pallas_call x1, Pallas kernels, token_gradient(): pl.pallas_call(back_kernel, out_shape=[like((rows, feats)), TOKEN], grid=...  2.61 us
    pallas_call x1, Pallas kernels, finish(): pl.pallas_call(finish_kernel, out_shape=[like((few, width))] + [like((row...  2.56 us
  transfers between devices with their start and end apart: 8, of which 3 were waited for; matrix products, arithmetic and copies ran while one was open for 0% of the time, Pallas kernels for 5%

profile of v2, /device:TPU:1, one launch (start us, length us, event | category | flops | bytes accessed | tf_op | source)
XLA Modules:
  0.0 111.4 jit_solution(14001532068375032981)
XLA Ops:
  0.6 0.9 copy-done.6
  1.5 0.1 shard_map.100
  1.6 0.0 copy-start.1
  1.7 29.0 %all_to_all.20 = bf16[12,128,512]{2,1,0:T(8,128)(2,1)S(1)} all-to-all(bf16[12,128,512]{2,1,0:T(8,128)(2,1)S(1)} %shard_map.100), channel_id=1, replica_groups=mesh['y'=8,'zh'=4,'c'=2,'zl'=3,'x'=4] {'zl','x'}, dimensions={0} | all-to-all | bytes 3145728 | tf_op jit(solution)/shard_map/all_to_all | solution.py:44
  30.6 1.8 %fusion.dep_ref = bf16[512,512]{1,0:T(8,128)(2,1)} fusion(bf16[1536,512]{1,0:T(8,128)(2,1)S(1)} %copy-done.1, bf16[1536,512]{1,0:T(8,128)(2,1)S(1)} %bitcast.7), kind=kOutput, calls=%fused_computation.1 | convolution fusion | flops 805830656 | bytes 3670016 | tf_op jit(solution)/shard_map/dot_general | solution.py:200
  32.4 14.2 %all-to-all-start.1 = ((bf16[16,32,512]{2,1,0:T(8,128)(2,1)}), bf16[16,32,512]{2,1,0:T(8,128)(2,1)S(1)}, u32[]{:S(2)}, u32[]{:S(2)}) async-start(bf16[16,32,512]{2,1,0:T(8,128)(2,1)} %bitcast.1), calls=%async_computation.1 | async-start | bytes 1048576 | tf_op jit(solution)/shard_map/all_to_all | solution.py:44
  46.7 0.0 copy-start.2
  46.7 1.4 %copy-done.2 = bf16[1536,512]{1,0:T(8,128)(2,1)S(1)} copy-done((bf16[1536,512]{1,0:T(8,128)(2,1)S(1)}, bf16[1536,512]{1,0:T(8,128)(2,1)}, u32[]{:S(2)}) %copy-start.2) | copy-done | bytes 1572888
  48.1 1.7 %shard_map.103 = (bf16[384,512]{1,0:T(8,128)(2,1)S(1)}, bf16[384,512]{1,0:T(8,128)(2,1)}, bf16[384,512]{1,0:T(8,128)(2,1)}, bf16[384,512]{1,0:T(8,128)(2,1)}) custom-call(s32[1]{0:T(128)} %bitcast.3.me_ref, bf16[1536,512]{1,0:T(8,128)(2,1)S(1)} %copy-done.2, f32[512,512]{1,0:T(8,128)S(1)} %copy-done, bf16[512,512]{1,0:T(8,128)(2,1)} %fusion.dep_ref), custom_call_target="tpu_custom_call" | custom-call | flops 1 | bytes 1 | tf_op jit(solution)/shard_map/pallas_call | solution.py:100
  49.8 2.4 %collective-permute-start = (bf16[384,512]{1,0:T(8,128)(2,1)}, bf16[384,512]{1,0:T(8,128)(2,1)}, u32[]{:S(2)}, u32[]{:S(2)}) collective-permute-start(bf16[384,512]{1,0:T(8,128)(2,1)} %get-tuple-element.28), channel_id=1, source_target_pairs={{0,1},{1,2},{2,3},{3,0},{4,5},{5,6},{6,7},{7,4},{8,9},{9,10},{10,1... | collective-permute-start | bytes 1179656 | tf_op jit(solution)/shard_map/ppermute | solution.py:161
  52.2 4.9 %collective-permute-start.1 = (bf16[384,512]{1,0:T(8,128)(2,1)}, bf16[384,512]{1,0:T(8,128)(2,1)}, u32[]{:S(2)}, u32[]{:S(2)}) collective-permute-start(bf16[384,512]{1,0:T(8,128)(2,1)} %get-tuple-element.29), channel_id=1, source_target_pairs={{0,2},{1,3},{2,0},{3,1},{4,6},{5,7},{6,4},{7,5},{8,10},{9,11},{10,... | collective-permute-start | bytes 1179656 | tf_op jit(solution)/shard_map/ppermute | solution.py:161
  57.1 2.2 %collective-permute-start.2 = (bf16[384,512]{1,0:T(8,128)(2,1)}, bf16[384,512]{1,0:T(8,128)(2,1)}, u32[]{:S(2)}, u32[]{:S(2)}) collective-permute-start(bf16[384,512]{1,0:T(8,128)(2,1)} %get-tuple-element.30), channel_id=1, source_target_pairs={{0,3},{1,0},{2,1},{3,2},{4,7},{5,4},{6,5},{7,6},{8,11},{9,8},{10,9... | collective-permute-start | bytes 1179656 | tf_op jit(solution)/shard_map/ppermute | solution.py:161
  59.3 2.1 %all-to-all-done.1.x_ref = bf16[16,32,512]{2,1,0:T(8,128)(2,1)S(1)} async-done(((bf16[16,32,512]{2,1,0:T(8,128)(2,1)}), bf16[16,32,512]{2,1,0:T(8,128)(2,1)S(1)}, u32[]{:S(2)}, u32[]{:S(2)}) %all-to-all-start.1) | async-done | bytes 524320 | tf_op jit(solution)/shard_map/all_to_all | solution.py:44
  61.4 0.1 shard_map.101
  61.5 0.0 copy-start.5
  61.5 0.6 copy-done.5
  62.2 14.2 %all-to-all-start.2 = ((bf16[4,32,512]{2,1,0:T(8,128)(2,1)}), bf16[4,32,512]{2,1,0:T(8,128)(2,1)S(1)}, u32[]{:S(2)}, u32[]{:S(2)}) async-start(bf16[4,32,512]{2,1,0:T(8,128)(2,1)} %copy-done.5), calls=%async_computation.2 | async-start | bytes 262144 | tf_op jit(solution)/shard_map/all_to_all | solution.py:44
  76.4 2.6 %shard_map.102 = (bf16[1536,512]{1,0:T(8,128)(2,1)}, f32[8,128]{1,0:T(8,128)S(1)}) custom-call(f32[8,128]{1,0:T(8,128)S(1)} %get-tuple-element.25.after_ref, bf16[1536,512]{1,0:T(8,128)(2,1)S(1)} %bitcast.8, f32[512,512]{1,0:T(8,128)S(1)} %copy-done), custom_call_target="tpu_custom_call" | custom-call | flops 1 | bytes 1 | tf_op jit(solution)/shard_map/pallas_call | solution.py:179
  79.0 0.0 collective-permute-done.refs_1_
  79.0 0.0 collective-permute-done.2.refs_3_
  79.0 1.5 %shard_map.104 = (f32[128,512]{1,0:T(8,128)S(1)}, bf16[128,512]{1,0:T(8,128)(2,1)S(1)}, bf16[128,512]{1,0:T(8,128)(2,1)S(1)}, f32[8,128]{1,0:T(8,128)S(1)}) custom-call(s32[1]{0:T(128)} %bitcast.2.me_ref, f32[8,128]{1,0:T(8,128)S(1)} %get-tuple-element.25.after_ref, bf16[384,512]{1,0:T(8,128)(2,1)S(1)} %get-tuple-element.27.refs_0_, ...), custom_call_target="tpu_custom_call" | custom-call | flops 1 | bytes 1 | tf_op jit(solution)/shard_map/pallas_call | solution.py:125
  80.5 5.7 %all-to-all-done.2.x_ref = bf16[4,32,512]{2,1,0:T(8,128)(2,1)S(1)} async-done(((bf16[4,32,512]{2,1,0:T(8,128)(2,1)}), bf16[4,32,512]{2,1,0:T(8,128)(2,1)S(1)}, u32[]{:S(2)}, u32[]{:S(2)}) %all-to-all-start.2) | async-done | bytes 131104 | tf_op jit(solution)/shard_map/all_to_all | solution.py:44
  86.3 0.7 shard_map.105
  87.0 6.0 %all-to-all-start.3 = ((bf16[8,32,512]{2,1,0:T(8,128)(2,1)}), bf16[8,32,512]{2,1,0:T(8,128)(2,1)S(1)}, u32[]{:S(2)}, u32[]{:S(2)}) async-start(bf16[8,32,512]{2,1,0:T(8,128)(2,1)} %get-tuple-element.32), calls=%async_computation.3 | async-start | bytes 524288 | tf_op jit(solution)/shard_map/all_to_all | solution.py:44
  93.0 4.1 %collective-permute-start.3 = (bf16[128,512]{1,0:T(8,128)(2,1)S(1)}, bf16[128,512]{1,0:T(8,128)(2,1)S(1)}, u32[]{:S(2)}, u32[]{:S(2)}) collective-permute-start(bf16[128,512]{1,0:T(8,128)(2,1)S(1)} %get-tuple-element.34), channel_id=1, source_target_pairs={{0,4},{4,8},{8,0},{1,5},{5,9},{9,1},{2,6},{6,10},{10,2},{3,7},{7,1... | collective-permute-start | bytes 393224 | tf_op jit(solution)/shard_map/ppermute | solution.py:161
  97.0 2.1 %collective-permute-start.4 = (bf16[128,512]{1,0:T(8,128)(2,1)S(1)}, bf16[128,512]{1,0:T(8,128)(2,1)S(1)}, u32[]{:S(2)}, u32[]{:S(2)}) collective-permute-start(bf16[128,512]{1,0:T(8,128)(2,1)S(1)} %get-tuple-element.35), channel_id=1, source_target_pairs={{0,8},{4,0},{8,4},{1,9},{5,1},{9,5},{2,10},{6,2},{10,6},{3,11},{7,... | collective-permute-start | bytes 393224 | tf_op jit(solution)/shard_map/ppermute | solution.py:161
  99.1 3.0 %all-to-all-done.3 = bf16[8,32,512]{2,1,0:T(8,128)(2,1)S(1)} async-done(((bf16[8,32,512]{2,1,0:T(8,128)(2,1)}), bf16[8,32,512]{2,1,0:T(8,128)(2,1)S(1)}, u32[]{:S(2)}, u32[]{:S(2)}) %all-to-all-start.3) | async-done | bytes 262176 | tf_op jit(solution)/shard_map/all_to_all | solution.py:44
  102.1 5.4 %all_gather.3.g_ref = bf16[512,512]{1,0:T(8,128)(2,1)S(1)} all-gather(bf16[256,512]{1,0:T(8,128)(2,1)S(1)} %bitcast.9), channel_id=1, replica_groups=mesh['y'=8,'zh'=4,'c'=2,'zl'=3,'x'=4] {'c'}, dimensions={0}, use_global_device_ids=true | all-gather | bytes 786432 | tf_op jit(solution)/shard_map/all_gather | solution.py:211
  107.6 0.0 collective-permute-done.4.c_ref
  107.6 0.0 copy-start.4
  107.6 1.2 %copy-done.4 = f32[512,512]{1,0:T(8,128)S(1)} copy-done((f32[512,512]{1,0:T(8,128)S(1)}, f32[512,512]{1,0:T(8,128)}, u32[]{:S(2)}) %copy-start.4) | copy-done | bytes 1048600
  108.8 2.6 %shard_map.106 = (bf16[128,512]{1,0:T(8,128)(2,1)}, f32[512,512]{1,0:T(8,128)}, f32[512,512]{1,0:T(8,128)}, f32[512,512]{1,0:T(8,128)}, f32[512,512]{1,0:T(8,128)}) custom-call(bf16[512,512]{1,0:T(8,128)(2,1)S(1)} %all_gather.3.g_ref, f32[512,512]{1,0:T(8,128)S(1)} %copy-done, f32[512,512]{1,0:T(8,128)S(1)} %copy-done.3, f32[512,512]{1,0:T(8,128)S(1)} %copy-done.4, ...), custom_call_target="tpu_custom_call" | custom-call | flops 1 | bytes 1 | tf_op jit(solution)/shard_map/pallas_call | solution.py:148
  (8 shorter events, 0.0 us)
Async XLA Ops:
  0.6 0.9 copy-start.6
  1.6 29.0 %copy-start.1 = (bf16[1536,512]{1,0:T(8,128)(2,1)S(1)}, bf16[1536,512]{1,0:T(8,128)(2,1)}, u32[]{:S(2)}) copy-start(bf16[1536,512]{1,0:T(8,128)(2,1)} %tokens_ref.1) | copy-start | bytes 4718596
  30.6 16.0 %copy-start = (f32[512,512]{1,0:T(8,128)S(1)}, f32[512,512]{1,0:T(8,128)}, u32[]{:S(2)}) copy-start(f32[512,512]{1,0:T(8,128)} %weight_ref.5) | copy-start | bytes 3145732
  32.4 29.0 %all-to-all-start.1 = ((bf16[16,32,512]{2,1,0:T(8,128)(2,1)}), bf16[16,32,512]{2,1,0:T(8,128)(2,1)S(1)}, u32[]{:S(2)}, u32[]{:S(2)}) async-start(bf16[16,32,512]{2,1,0:T(8,128)(2,1)} %bitcast.1), calls=%async_computation.1 | async-start | bytes 1048576 | tf_op jit(solution)/shard_map/all_to_all | solution.py:44
  46.7 1.4 %copy-start.2 = (bf16[1536,512]{1,0:T(8,128)(2,1)S(1)}, bf16[1536,512]{1,0:T(8,128)(2,1)}, u32[]{:S(2)}) copy-start(bf16[1536,512]{1,0:T(8,128)(2,1)} %tokens_ref.1) | copy-start | bytes 4718596
  49.8 29.2 %collective-permute-start = (bf16[384,512]{1,0:T(8,128)(2,1)}, bf16[384,512]{1,0:T(8,128)(2,1)}, u32[]{:S(2)}, u32[]{:S(2)}) collective-permute-start(bf16[384,512]{1,0:T(8,128)(2,1)} %get-tuple-element.28), channel_id=1, source_target_pairs={{0,1},{1,2},{2,3},{3,0},{4,5},{5,6},{6,7},{7,4},{8,9},{9,10},{10,1... | collective-permute-start | bytes 1179656 | tf_op jit(solution)/shard_map/ppermute | solution.py:161
  52.2 26.8 %collective-permute-start.1 = (bf16[384,512]{1,0:T(8,128)(2,1)}, bf16[384,512]{1,0:T(8,128)(2,1)}, u32[]{:S(2)}, u32[]{:S(2)}) collective-permute-start(bf16[384,512]{1,0:T(8,128)(2,1)} %get-tuple-element.29), channel_id=1, source_target_pairs={{0,2},{1,3},{2,0},{3,1},{4,6},{5,7},{6,4},{7,5},{8,10},{9,11},{10,... | collective-permute-start | bytes 1179656 | tf_op jit(solution)/shard_map/ppermute | solution.py:161
  57.1 21.9 %collective-permute-start.2 = (bf16[384,512]{1,0:T(8,128)(2,1)}, bf16[384,512]{1,0:T(8,128)(2,1)}, u32[]{:S(2)}, u32[]{:S(2)}) collective-permute-start(bf16[384,512]{1,0:T(8,128)(2,1)} %get-tuple-element.30), channel_id=1, source_target_pairs={{0,3},{1,0},{2,1},{3,2},{4,7},{5,4},{6,5},{7,6},{8,11},{9,8},{10,9... | collective-permute-start | bytes 1179656 | tf_op jit(solution)/shard_map/ppermute | solution.py:161
  61.5 0.7 copy-start.5
  62.2 24.1 %all-to-all-start.2 = ((bf16[4,32,512]{2,1,0:T(8,128)(2,1)}), bf16[4,32,512]{2,1,0:T(8,128)(2,1)S(1)}, u32[]{:S(2)}, u32[]{:S(2)}) async-start(bf16[4,32,512]{2,1,0:T(8,128)(2,1)} %copy-done.5), calls=%async_computation.2 | async-start | bytes 262144 | tf_op jit(solution)/shard_map/all_to_all | solution.py:44
  79.0 28.6 %copy-start.3 = (f32[512,512]{1,0:T(8,128)S(1)}, f32[512,512]{1,0:T(8,128)}, u32[]{:S(2)}) copy-start(f32[512,512]{1,0:T(8,128)} %moment_ref.1) | copy-start | bytes 3145732
  87.0 15.1 %all-to-all-start.3 = ((bf16[8,32,512]{2,1,0:T(8,128)(2,1)}), bf16[8,32,512]{2,1,0:T(8,128)(2,1)S(1)}, u32[]{:S(2)}, u32[]{:S(2)}) async-start(bf16[8,32,512]{2,1,0:T(8,128)(2,1)} %get-tuple-element.32), calls=%async_computation.3 | async-start | bytes 524288 | tf_op jit(solution)/shard_map/all_to_all | solution.py:44
  93.0 14.6 %collective-permute-start.3 = (bf16[128,512]{1,0:T(8,128)(2,1)S(1)}, bf16[128,512]{1,0:T(8,128)(2,1)S(1)}, u32[]{:S(2)}, u32[]{:S(2)}) collective-permute-start(bf16[128,512]{1,0:T(8,128)(2,1)S(1)} %get-tuple-element.34), channel_id=1, source_target_pairs={{0,4},{4,8},{8,0},{1,5},{5,9},{9,1},{2,6},{6,10},{10,2},{3,7},{7,1... | collective-permute-start | bytes 393224 | tf_op jit(solution)/shard_map/ppermute | solution.py:161
  97.0 10.6 %collective-permute-start.4 = (bf16[128,512]{1,0:T(8,128)(2,1)S(1)}, bf16[128,512]{1,0:T(8,128)(2,1)S(1)}, u32[]{:S(2)}, u32[]{:S(2)}) collective-permute-start(bf16[128,512]{1,0:T(8,128)(2,1)S(1)} %get-tuple-element.35), channel_id=1, source_target_pairs={{0,8},{4,0},{8,4},{1,9},{5,1},{9,5},{2,10},{6,2},{10,6},{3,11},{7,... | collective-permute-start | bytes 393224 | tf_op jit(solution)/shard_map/ppermute | solution.py:161
  107.6 1.2 %copy-start.4 = (f32[512,512]{1,0:T(8,128)S(1)}, f32[512,512]{1,0:T(8,128)}, u32[]{:S(2)}) copy-start(f32[512,512]{1,0:T(8,128)} %second_ref.1) | copy-start | bytes 3145732

commit v3 on v2

--- a/solution.py
+++ b/solution.py
@@ -11,7 +11,6 @@
 AXES = ("y", "zh", "c", "zl", "x")
 DP = ("y", "zh", "c")
 BLK = ("zl", "x")
-PAIR = ("c", "y")
 BRIEF = pl.CostEstimate(flops=1, bytes_accessed=1, transcendentals=0)
 BF16, F32 = jnp.bfloat16, jnp.float32
 VMEM = pl.BlockSpec(memory_space=pltpu.VMEM)
@@ -82,7 +81,7 @@
     )(x, *tokens)
 
 
-def partial_kernel(me_ref, tokens_ref, weight_ref, dep_ref, *outs):
+def partial_kernel(me_ref, tokens_ref, weight_ref, *outs):
     count = len(outs)
     groups = 3
     rows = tokens_ref.shape[0] // (count * groups)
@@ -95,16 +94,16 @@
         out[...] = jnp.dot(block, scaled, preferred_element_type=F32).astype(out.dtype)
 
 
-def partial_keys(tokens, weight, count, dep):
+def partial_keys(tokens, weight, count):
     rows, width = tokens.shape[0] // count, weight.shape[1]
     return pl.pallas_call(
         partial_kernel,
         out_shape=[like((rows, width))] * count,
-        in_specs=[SMEM, VMEM, VMEM, ANY],
+        in_specs=[SMEM, VMEM, VMEM],
         out_specs=[VMEM] * count,
         compiler_params=params(16),
         cost_estimate=BRIEF,
-    )(lax.axis_index("x").reshape(1), tokens, weight, dep)
+    )(lax.axis_index("x").reshape(1), tokens, weight)
 
 
 def ring_sum_kernel(me_ref, after_ref, *refs):
@@ -132,28 +131,40 @@
     )(lax.axis_index("zl").reshape(1), token, *parts)
 
 
-def finish_kernel(g_ref, weight_ref, moment_ref, second_ref, a_ref, b_ref, c_ref, *outs):
-    grad = g_ref[...].astype(F32)
-    new = optimize(weight_ref[...], moment_ref[...], second_ref[...], grad)
-    keys = (a_ref[...] + b_ref[...].astype(F32) + c_ref[...].astype(F32)).astype(BF16)
-    for out, value in zip(outs, (keys, grad) + new, strict=True):
-        out[...] = value
-
-
-def finish(grad, weight, moment, second, parts):
-    (rows, width), (few, _) = grad.shape, parts[0].shape
-    steps = 4
-    big = pl.BlockSpec((rows // steps, width), lambda i: (i, 0))
-    small = pl.BlockSpec((few // steps, width), lambda i: (i, 0))
-    return pl.pallas_call(
-        finish_kernel,
-        out_shape=[like((few, width))] + [like((rows, width), F32)] * 4,
-        grid=(steps,),
-        in_specs=[big] * 4 + [small] * 3,
-        out_specs=[small] + [big] * 4,
-        compiler_params=params(16),
-        cost_estimate=BRIEF,
-    )(grad, weight, moment, second, *parts)
+def pair_kernel(me_ref, grad_ref, got_ref, after_ref, o_ref):
+    me = me_ref[0]
+    rows = o_ref.shape[0]
+    mine = grad_ref[pl.ds(pl.multiple_of(me * rows, rows), rows), :].astype(F32)
+    o_ref[...] = (mine + got_ref[1 - me].astype(F32)).astype(o_ref.dtype)
+
+
+def pair_sum(grad, token):
+    rows, width = grad.shape[0] // 2, grad.shape[1]
+    core = lax.axis_index("c")
+    got = lax.all_gather(lax.dynamic_slice_in_dim(grad, (1 - core) * rows, rows, 0), "c", axis=0)
+    return pl.pallas_call(
+        pair_kernel,
+        out_shape=like((rows, width)),
+        in_specs=[SMEM, VMEM, VMEM, ANY],
+        out_specs=VMEM,
+        compiler_params=params(8),
+        cost_estimate=BRIEF,
+    )(core.reshape(1), grad, got, token)
+
+
+def last_sum_kernel(a_ref, b_ref, c_ref, after_ref, o_ref):
+    o_ref[...] = (a_ref[...] + b_ref[...].astype(F32) + c_ref[...].astype(F32)).astype(o_ref.dtype)
+
+
+def last_sum(a, b, c, token):
+    return pl.pallas_call(
+        last_sum_kernel,
+        out_shape=like(a.shape),
+        in_specs=[VMEM] * 3 + [ANY],
+        out_specs=VMEM,
+        compiler_params=params(4),
+        cost_estimate=BRIEF,
+    )(a, b, c, token)
 
 
 def send(x, axis, shift):
@@ -199,18 +210,21 @@
 
     grad = lax.dot_general(tokens, piece, (((0,), (0,)), ((), ())), preferred_element_type=F32) * FACTOR
     grad = grad.astype(BF16)
-    own, *out = partial_keys(tokens, weight, size("x"), grad)
+    own, *out = partial_keys(tokens, weight, size("x"))
     got = [send(x, "x", 1 + i) for i, x in enumerate(out)]
-    pair = size("y") * size("c")
-    shares, first = sum_copies(swap_parts(grad.reshape(pair, feats // pair, width), PAIR), size("zh"))
+    pair = pair_sum(grad, got[0])
+    shares = swap_parts(pair.reshape(size("y"), -1, width), "y")
+    shares, first = sum_copies(shares, size("zh"))
     back, after_back = token_gradient(piece, weight, first)
     mine, *out, after_keys = ring_sum([own] + got, first)
     got = [send(x, "zl", 1 + i) for i, x in enumerate(out)]
     shares, _ = sum_copies(swap_parts(shares, "zh"), size("y"), after_back, after_keys)
-    half = swap_parts(shares, "y").reshape(feats // size("c"), width)
-    full = lax.all_gather(half, "c", axis=0, tiled=True)
-    keys, weight_grad, *new = finish(full, weight, moment, second, [mine] + got)
-    return (keys, back, weight_grad, *new)
+    half = swap_parts(shares, "y").reshape(pair.shape)
+    weight_grad = lax.all_gather(half, "c", axis=0, tiled=True).astype(F32)
+
+    keys = last_sum(mine, *got, half)
+    weight_new, moment_new, second_new = optimize(weight, moment, second, weight_grad)
+    return (keys, back, weight_grad, weight_new, moment_new, second_new)
 
 
 def solution(mesh):

time: 112 us -> 112 us (level)
  blocking collectives: 34.4 us -> 19.6 us
  waiting for transfers between devices: 10.8 us -> 24.8 us
  other arithmetic: 0 us -> 3.92 us
  starting transfers between devices: 50.1 us -> 46.5 us
  local copies, waits for them, and re-layouts: 4.18 us -> 6.35 us
  Pallas kernels: 9.32 us -> 7.23 us
    all_to_all x1 -> x0, blocking collectives: 29 us -> none  [swap_parts(): return lax.all_to_all(x, axes, 0, 0, tiled=True)]
    all_gather x1 -> x2, blocking collectives: 5.44 us -> 19.6 us  [the longest x1 13.8 us: pair_sum(): lax.all_gather(lax.dynamic_slice_in_dim(grad, (1 - core) * rows, rows, 0)...]
    all_to_all x3 -> x4, waiting for transfers between devices: 10.8 us -> 24.8 us  [swap_parts(): return lax.all_to_all(x, axes, 0, 0, tiled=True)]
    sub x0 -> x1, other arithmetic: none -> 3.92 us  [optimize(): weight_new = weight - 0.05 * (step_dir + 0.1 * weight)]
    all_to_all x3 -> x4, starting transfers between devices: 34.4 us -> 31.4 us  [swap_parts(): return lax.all_to_all(x, axes, 0, 0, tiled=True)]
    unnamed x14 -> x18, local copies, waits for them, and re-layouts: 4.18 us -> 6.33 us
    pallas_call x1 -> x2, Pallas kernels: 2.56 us -> 1.46 us  [the longest x1 0.77 us: pair_sum(): pl.pallas_call(pair_kernel, out_shape=like((rows, width)), in_specs=[SMEM...]
  transfers between devices with their start and end apart: 8 -> 9, of which waited for: 3 -> 4; matrix products, arithmetic and copies ran while one was open for 0% -> 6% of each run, Pallas kernels for 5% -> 4%
where the time goes in v3:
time: 112 us
  starting transfers between devices  46.5 us (42%)
  waiting for transfers between devices  24.8 us (22%)
  blocking collectives  19.6 us (18%)
  Pallas kernels  7.23 us (6%)
  local copies, waits for them, and re-layouts  6.35 us (6%)
  other arithmetic  3.92 us (4%)
  matrix products  2.41 us (2%)
    all_to_all x4, starting transfers between devices, swap_parts(): return lax.all_to_all(x, axes, 0, 0, tiled=True)  31.4 us
    all_to_all x4, waiting for transfers between devices, swap_parts(): return lax.all_to_all(x, axes, 0, 0, tiled=True)  24.8 us
    ppermute x5, starting transfers between devices, send(): lax.ppermute(x, axis, [(i, (i + shift) % count) for i in range(count)])  15.1 us
    all_gather x1, blocking collectives, pair_sum(): lax.all_gather(lax.dynamic_slice_in_dim(grad, (1 - core) * rows, rows, 0)...  13.8 us
    unnamed x18, local copies, waits for them, and re-layouts  6.33 us
    all_gather x1, blocking collectives, local(): weight_grad = lax.all_gather(half, 'c', axis=0, tiled=True).astype(F32)  5.79 us
    sub x1, other arithmetic, optimize(): weight_new = weight - 0.05 * (step_dir + 0.1 * weight)  3.92 us
    pallas_call x1, Pallas kernels, token_gradient(): pl.pallas_call(back_kernel, out_shape=[like((rows, feats)), TOKEN], grid=...  2.61 us
  transfers between devices with their start and end apart: 9, of which 4 were waited for; matrix products, arithmetic and copies ran while one was open for 6% of the time, Pallas kernels for 4%

profile of v3, /device:TPU:1, one launch (start us, length us, event | category | flops | bytes accessed | tf_op | source)
XLA Modules:
  0.0 111.6 jit_solution(14666277063439281565)
XLA Ops:
  0.6 0.9 copy-done.6
  1.5 0.1 shard_map.100
  1.6 0.0 copy-start.2
  1.7 1.1 %copy-done.2 = bf16[12,128,512]{2,1,0:T(8,128)(2,1)} copy-done((bf16[12,128,512]{2,1,0:T(8,128)(2,1)}, bf16[12,128,512]{2,1,0:T(8,128)(2,1)S(1)}, u32[]{:S(2)}) %copy-start.2) | copy-done | bytes 1572888
  2.8 8.6 %all-to-all-start = ((bf16[12,128,512]{2,1,0:T(8,128)(2,1)}), bf16[12,128,512]{2,1,0:T(8,128)(2,1)S(1)}, u32[]{:S(2)}, u32[]{:S(2)}) async-start(bf16[12,128,512]{2,1,0:T(8,128)(2,1)} %copy-done.2), calls=%async_computation | async-start | bytes 3145728 | tf_op jit(solution)/shard_map/all_to_all | solution.py:43
  11.5 1.4 %copy-done.1 = bf16[1536,512]{1,0:T(8,128)(2,1)S(1)} copy-done((bf16[1536,512]{1,0:T(8,128)(2,1)S(1)}, bf16[1536,512]{1,0:T(8,128)(2,1)}, u32[]{:S(2)}) %copy-start.1) | copy-done | bytes 1572888
  12.9 1.0 shard_map.101
  13.9 0.7 copy-done.3
  14.6 0.7 copy-done.7
  15.3 0.7 copy-done.8
  16.1 3.3 %collective-permute-start = (bf16[384,512]{1,0:T(8,128)(2,1)S(1)}, bf16[384,512]{1,0:T(8,128)(2,1)S(1)}, u32[]{:S(2)}, u32[]{:S(2)}) collective-permute-start(bf16[384,512]{1,0:T(8,128)(2,1)S(1)} %get-tuple-element.19), channel_id=1, source_target_pairs={{0,1},{1,2},{2,3},{3,0},{4,5},{5,6},{6,7},{7,4},{8,9},{9,10},{10,1... | collective-permute-start | bytes 1179656 | tf_op jit(solution)/shard_map/ppermute | solution.py:172
  19.4 9.5 %all-to-all-done = bf16[12,128,512]{2,1,0:T(8,128)(2,1)S(1)} async-done(((bf16[12,128,512]{2,1,0:T(8,128)(2,1)}), bf16[12,128,512]{2,1,0:T(8,128)(2,1)S(1)}, u32[]{:S(2)}, u32[]{:S(2)}) %all-to-all-start) | async-done | bytes 1572896 | tf_op jit(solution)/shard_map/all_to_all | solution.py:43
  28.9 2.4 %fusion.grad_ref = bf16[512,512]{1,0:T(8,128)(2,1)S(1)} fusion(bf16[1536,512]{1,0:T(8,128)(2,1)} %tokens_ref.1, bf16[1536,512]{1,0:T(8,128)(2,1)S(1)} %bitcast.9), kind=kOutput, calls=%fused_computation.2 | convolution fusion | flops 805830656 | bytes 3670016 | tf_op jit(solution)/shard_map/dot_general | solution.py:211
  31.4 13.8 %all-gather = bf16[512,512]{1,0:T(8,128)(2,1)S(1)} all-gather(bf16[256,512]{1,0:T(8,128)(2,1)S(1)} %constant_dynamic-slice_fusion), channel_id=2, replica_groups=mesh['y'=8,'zh'=4,'c'=2,'zl'=3,'x'=4] {'c'}, dimensions={0}, use_global_device_ids=true | all-gather | bytes 786432 | tf_op jit(solution)/shard_map/all_gather | solution.py:144
  45.2 0.8 shard_map.102
  45.9 6.4 %all-to-all-start.1 = ((bf16[8,32,512]{2,1,0:T(8,128)(2,1)}), bf16[8,32,512]{2,1,0:T(8,128)(2,1)S(1)}, u32[]{:S(2)}, u32[]{:S(2)}) async-start(bf16[8,32,512]{2,1,0:T(8,128)(2,1)} %bitcast.5), calls=%async_computation.1 | async-start | bytes 524288 | tf_op jit(solution)/shard_map/all_to_all | solution.py:43
  52.3 2.5 %collective-permute-start.1 = (bf16[384,512]{1,0:T(8,128)(2,1)}, bf16[384,512]{1,0:T(8,128)(2,1)}, u32[]{:S(2)}, u32[]{:S(2)}) collective-permute-start(bf16[384,512]{1,0:T(8,128)(2,1)} %copy-done.8), channel_id=1, source_target_pairs={{0,2},{1,3},{2,0},{3,1},{4,6},{5,7},{6,4},{7,5},{8,10},{9,11},{10,... | collective-permute-start | bytes 1179656 | tf_op jit(solution)/shard_map/ppermute | solution.py:172
  54.8 3.2 %collective-permute-start.2 = (bf16[384,512]{1,0:T(8,128)(2,1)}, bf16[384,512]{1,0:T(8,128)(2,1)}, u32[]{:S(2)}, u32[]{:S(2)}) collective-permute-start(bf16[384,512]{1,0:T(8,128)(2,1)} %copy-done.7), channel_id=1, source_target_pairs={{0,3},{1,0},{2,1},{3,2},{4,7},{5,4},{6,5},{7,6},{8,11},{9,8},{10,9... | collective-permute-start | bytes 1179656 | tf_op jit(solution)/shard_map/ppermute | solution.py:172
  58.0 5.4 %all-to-all-done.1.x_ref = bf16[8,32,512]{2,1,0:T(8,128)(2,1)S(1)} async-done(((bf16[8,32,512]{2,1,0:T(8,128)(2,1)}), bf16[8,32,512]{2,1,0:T(8,128)(2,1)S(1)}, u32[]{:S(2)}, u32[]{:S(2)}) %all-to-all-start.1) | async-done | bytes 262176 | tf_op jit(solution)/shard_map/all_to_all | solution.py:43
  63.4 0.6 copy-done.5
  64.1 13.0 %all-to-all-start.2 = ((bf16[4,32,512]{2,1,0:T(8,128)(2,1)}), bf16[4,32,512]{2,1,0:T(8,128)(2,1)S(1)}, u32[]{:S(2)}, u32[]{:S(2)}) async-start(bf16[4,32,512]{2,1,0:T(8,128)(2,1)} %copy-done.5), calls=%async_computation.2 | async-start | bytes 262144 | tf_op jit(solution)/shard_map/all_to_all | solution.py:43
  77.1 2.6 %shard_map.105 = (bf16[1536,512]{1,0:T(8,128)(2,1)}, f32[8,128]{1,0:T(8,128)S(1)}) custom-call(f32[8,128]{1,0:T(8,128)S(1)} %get-tuple-element.20.after_ref, bf16[1536,512]{1,0:T(8,128)(2,1)S(1)} %bitcast.10, f32[512,512]{1,0:T(8,128)S(1)} %copy-done), custom_call_target="tpu_custom_call" | custom-call | flops 1 | bytes 1 | tf_op jit(solution)/shard_map/pallas_call | solution.py:190
  79.7 1.3 %shard_map.104 = (f32[128,512]{1,0:T(8,128)S(1)}, bf16[128,512]{1,0:T(8,128)(2,1)S(1)}, bf16[128,512]{1,0:T(8,128)(2,1)S(1)}, f32[8,128]{1,0:T(8,128)S(1)}) custom-call(s32[1]{0:T(128)} %bitcast.me_ref, f32[8,128]{1,0:T(8,128)S(1)} %get-tuple-element.20.after_ref, bf16[384,512]{1,0:T(8,128)(2,1)S(1)} %copy-done.4, ...), custom_call_target="tpu_custom_call" | custom-call | flops 1 | bytes 1 | tf_op jit(solution)/shard_map/pallas_call | solution.py:124
  81.0 6.7 %all-to-all-done.2.x_ref = bf16[4,32,512]{2,1,0:T(8,128)(2,1)S(1)} async-done(((bf16[4,32,512]{2,1,0:T(8,128)(2,1)}), bf16[4,32,512]{2,1,0:T(8,128)(2,1)S(1)}, u32[]{:S(2)}, u32[]{:S(2)}) %all-to-all-start.2) | async-done | bytes 131104 | tf_op jit(solution)/shard_map/all_to_all | solution.py:43
  87.7 0.7 shard_map.106
  88.4 3.4 %all-to-all-start.3 = ((bf16[8,32,512]{2,1,0:T(8,128)(2,1)}), bf16[8,32,512]{2,1,0:T(8,128)(2,1)S(1)}, u32[]{:S(2)}, u32[]{:S(2)}) async-start(bf16[8,32,512]{2,1,0:T(8,128)(2,1)} %get-tuple-element.30), calls=%async_computation.3 | async-start | bytes 524288 | tf_op jit(solution)/shard_map/all_to_all | solution.py:43
  91.9 2.2 %collective-permute-start.3 = (bf16[128,512]{1,0:T(8,128)(2,1)S(1)}, bf16[128,512]{1,0:T(8,128)(2,1)S(1)}, u32[]{:S(2)}, u32[]{:S(2)}) collective-permute-start(bf16[128,512]{1,0:T(8,128)(2,1)S(1)} %get-tuple-element.25), channel_id=1, source_target_pairs={{0,4},{4,8},{8,0},{1,5},{5,9},{9,1},{2,6},{6,10},{10,2},{3,7},{7,1... | collective-permute-start | bytes 393224 | tf_op jit(solution)/shard_map/ppermute | solution.py:172
  94.1 4.0 %collective-permute-start.4 = (bf16[128,512]{1,0:T(8,128)(2,1)S(1)}, bf16[128,512]{1,0:T(8,128)(2,1)S(1)}, u32[]{:S(2)}, u32[]{:S(2)}) collective-permute-start(bf16[128,512]{1,0:T(8,128)(2,1)S(1)} %get-tuple-element.26), channel_id=1, source_target_pairs={{0,8},{4,0},{8,4},{1,9},{5,1},{9,5},{2,10},{6,2},{10,6},{3,11},{7,... | collective-permute-start | bytes 393224 | tf_op jit(solution)/shard_map/ppermute | solution.py:172
  98.1 3.1 %all-to-all-done.3 = bf16[8,32,512]{2,1,0:T(8,128)(2,1)S(1)} async-done(((bf16[8,32,512]{2,1,0:T(8,128)(2,1)}), bf16[8,32,512]{2,1,0:T(8,128)(2,1)S(1)}, u32[]{:S(2)}, u32[]{:S(2)}) %all-to-all-start.3) | async-done | bytes 262176 | tf_op jit(solution)/shard_map/all_to_all | solution.py:43
  101.2 5.8 %all_gather.11 = bf16[512,512]{1,0:T(8,128)(2,1)S(1)} all-gather(bf16[256,512]{1,0:T(8,128)(2,1)S(1)} %bitcast.11), channel_id=1, replica_groups=mesh['y'=8,'zh'=4,'c'=2,'zl'=3,'x'=4] {'c'}, dimensions={0}, use_global_device_ids=true | all-gather | bytes 786432 | tf_op jit(solution)/shard_map/all_gather | solution.py:223
  107.0 3.9 %multiply_subtract_fusion = (f32[512,512]{1,0:T(8,128)}, f32[512,512]{1,0:T(8,128)}, f32[512,512]{1,0:T(8,128)}, f32[512,512]{1,0:T(8,128)}) fusion(f32[512,512]{1,0:T(8,128)S(1)} %copy-done, f32[512,512]{1,0:T(8,128)} %param.8, f32[512,512]{1,0:T(8,128)} %param.9, bf16[512,512]{1,0:T(8,128)(2,1)S(1)} %all_gather.11), kind=kLoop, calls=%fused_computation.4 | loop fusion | flops 4194304 | bytes 7864320 | tf_op jit(solution)/shard_map/sub | solution.py:27
  110.9 0.7 shard_map.107
  (17 shorter events, 0.1 us)
Async XLA Ops:
  0.6 0.9 copy-start.6
  1.6 1.1 %copy-start.2 = (bf16[12,128,512]{2,1,0:T(8,128)(2,1)}, bf16[12,128,512]{2,1,0:T(8,128)(2,1)S(1)}, u32[]{:S(2)}) copy-start(bf16[12,128,512]{2,1,0:T(8,128)(2,1)S(1)} %shard_map.100) | copy-start | bytes 4718596
  2.8 8.6 %copy-start = (f32[512,512]{1,0:T(8,128)S(1)}, f32[512,512]{1,0:T(8,128)}, u32[]{:S(2)}) copy-start(f32[512,512]{1,0:T(8,128)} %weight_ref.3) | copy-start | bytes 3145732
  2.8 26.2 %all-to-all-start = ((bf16[12,128,512]{2,1,0:T(8,128)(2,1)}), bf16[12,128,512]{2,1,0:T(8,128)(2,1)S(1)}, u32[]{:S(2)}, u32[]{:S(2)}) async-start(bf16[12,128,512]{2,1,0:T(8,128)(2,1)} %copy-done.2), calls=%async_computation | async-start | bytes 3145728 | tf_op jit(solution)/shard_map/all_to_all | solution.py:43
  11.4 1.4 %copy-start.1 = (bf16[1536,512]{1,0:T(8,128)(2,1)S(1)}, bf16[1536,512]{1,0:T(8,128)(2,1)}, u32[]{:S(2)}) copy-start(bf16[1536,512]{1,0:T(8,128)(2,1)} %tokens_ref.1) | copy-start | bytes 4718596
  13.8 0.7 copy-start.3
  14.6 0.7 copy-start.7
  15.3 0.7 copy-start.8
  16.1 29.1 %collective-permute-start = (bf16[384,512]{1,0:T(8,128)(2,1)S(1)}, bf16[384,512]{1,0:T(8,128)(2,1)S(1)}, u32[]{:S(2)}, u32[]{:S(2)}) collective-permute-start(bf16[384,512]{1,0:T(8,128)(2,1)S(1)} %get-tuple-element.19), channel_id=1, source_target_pairs={{0,1},{1,2},{2,3},{3,0},{4,5},{5,6},{6,7},{7,4},{8,9},{9,10},{10,1... | collective-permute-start | bytes 1179656 | tf_op jit(solution)/shard_map/ppermute | solution.py:172
  45.9 17.5 %all-to-all-start.1 = ((bf16[8,32,512]{2,1,0:T(8,128)(2,1)}), bf16[8,32,512]{2,1,0:T(8,128)(2,1)S(1)}, u32[]{:S(2)}, u32[]{:S(2)}) async-start(bf16[8,32,512]{2,1,0:T(8,128)(2,1)} %bitcast.5), calls=%async_computation.1 | async-start | bytes 524288 | tf_op jit(solution)/shard_map/all_to_all | solution.py:43
  52.3 27.4 %collective-permute-start.1 = (bf16[384,512]{1,0:T(8,128)(2,1)}, bf16[384,512]{1,0:T(8,128)(2,1)}, u32[]{:S(2)}, u32[]{:S(2)}) collective-permute-start(bf16[384,512]{1,0:T(8,128)(2,1)} %copy-done.8), channel_id=1, source_target_pairs={{0,2},{1,3},{2,0},{3,1},{4,6},{5,7},{6,4},{7,5},{8,10},{9,11},{10,... | collective-permute-start | bytes 1179656 | tf_op jit(solution)/shard_map/ppermute | solution.py:172
  54.8 24.9 %collective-permute-start.2 = (bf16[384,512]{1,0:T(8,128)(2,1)}, bf16[384,512]{1,0:T(8,128)(2,1)}, u32[]{:S(2)}, u32[]{:S(2)}) collective-permute-start(bf16[384,512]{1,0:T(8,128)(2,1)} %copy-done.7), channel_id=1, source_target_pairs={{0,3},{1,0},{2,1},{3,2},{4,7},{5,4},{6,5},{7,6},{8,11},{9,8},{10,9... | collective-permute-start | bytes 1179656 | tf_op jit(solution)/shard_map/ppermute | solution.py:172
  63.4 0.7 copy-start.5
  64.1 15.6 %copy-start.4 = (bf16[384,512]{1,0:T(8,128)(2,1)S(1)}, bf16[384,512]{1,0:T(8,128)(2,1)}, u32[]{:S(2)}) copy-start(bf16[384,512]{1,0:T(8,128)(2,1)} %copy-done.3) | copy-start | bytes 1179652
  64.1 23.6 %all-to-all-start.2 = ((bf16[4,32,512]{2,1,0:T(8,128)(2,1)}), bf16[4,32,512]{2,1,0:T(8,128)(2,1)S(1)}, u32[]{:S(2)}, u32[]{:S(2)}) async-start(bf16[4,32,512]{2,1,0:T(8,128)(2,1)} %copy-done.5), calls=%async_computation.2 | async-start | bytes 262144 | tf_op jit(solution)/shard_map/all_to_all | solution.py:43
  88.4 12.7 %all-to-all-start.3 = ((bf16[8,32,512]{2,1,0:T(8,128)(2,1)}), bf16[8,32,512]{2,1,0:T(8,128)(2,1)S(1)}, u32[]{:S(2)}, u32[]{:S(2)}) async-start(bf16[8,32,512]{2,1,0:T(8,128)(2,1)} %get-tuple-element.30), calls=%async_computation.3 | async-start | bytes 524288 | tf_op jit(solution)/shard_map/all_to_all | solution.py:43
  91.9 19.0 %collective-permute-start.3 = (bf16[128,512]{1,0:T(8,128)(2,1)S(1)}, bf16[128,512]{1,0:T(8,128)(2,1)S(1)}, u32[]{:S(2)}, u32[]{:S(2)}) collective-permute-start(bf16[128,512]{1,0:T(8,128)(2,1)S(1)} %get-tuple-element.25), channel_id=1, source_target_pairs={{0,4},{4,8},{8,0},{1,5},{5,9},{9,1},{2,6},{6,10},{10,2},{3,7},{7,1... | collective-permute-start | bytes 393224 | tf_op jit(solution)/shard_map/ppermute | solution.py:172
  94.1 16.8 %collective-permute-start.4 = (bf16[128,512]{1,0:T(8,128)(2,1)S(1)}, bf16[128,512]{1,0:T(8,128)(2,1)S(1)}, u32[]{:S(2)}, u32[]{:S(2)}) collective-permute-start(bf16[128,512]{1,0:T(8,128)(2,1)S(1)} %get-tuple-element.26), channel_id=1, source_target_pairs={{0,8},{4,0},{8,4},{1,9},{5,1},{9,5},{2,10},{6,2},{10,6},{3,11},{7,... | collective-permute-start | bytes 393224 | tf_op jit(solution)/shard_map/ppermute | solution.py:172

commit v4 on v3

--- a/solution.py
+++ b/solution.py
@@ -11,6 +11,7 @@
 AXES = ("y", "zh", "c", "zl", "x")
 DP = ("y", "zh", "c")
 BLK = ("zl", "x")
+CROSS = ("x", "zl")
 BRIEF = pl.CostEstimate(flops=1, bytes_accessed=1, transcendentals=0)
 BF16, F32 = jnp.bfloat16, jnp.float32
 VMEM = pl.BlockSpec(memory_space=pltpu.VMEM)
@@ -81,10 +82,14 @@
     )(x, *tokens)
 
 
-def partial_kernel(me_ref, tokens_ref, weight_ref, *outs):
+def partial_kernel(me_ref, tokens_ref, weight_ref, held_ref, *outs):
     count = len(outs)
     groups = 3
     rows = tokens_ref.shape[0] // (count * groups)
+    for x in range(count):
+        for g in range(groups):
+            to, at = (x * groups + g) * rows, (g * count + x) * rows
+            held_ref[to : to + rows, :] = tokens_ref[at : at + rows, :]
     scaled = (weight_ref[...] * FACTOR).astype(BF16)
     for shift, out in enumerate(outs):
         at = lax.rem(me_ref[0] + shift, count)
@@ -98,9 +103,9 @@
     rows, width = tokens.shape[0] // count, weight.shape[1]
     return pl.pallas_call(
         partial_kernel,
-        out_shape=[like((rows, width))] * count,
+        out_shape=[like(tokens.shape)] + [like((rows, width))] * count,
         in_specs=[SMEM, VMEM, VMEM],
-        out_specs=[VMEM] * count,
+        out_specs=[VMEM] * (count + 1),
         compiler_params=params(16),
         cost_estimate=BRIEF,
     )(lax.axis_index("x").reshape(1), tokens, weight)
@@ -179,21 +184,21 @@
         token_ref[...] = jnp.zeros(token_ref.shape, F32)
 
     o_ref[...] = lax.dot_general(
-        piece_ref[...], scaled_ref[...], (((1,), (1,)), ((), ())), preferred_element_type=F32
+        piece_ref[...].reshape(o_ref.shape[0], -1), scaled_ref[...], (((1,), (1,)), ((), ())), preferred_element_type=F32
     ).astype(o_ref.dtype)
 
 
 def token_gradient(piece, weight, token):
-    rows, width = piece.shape
+    wide, tall, own, width = piece.shape
     feats = weight.shape[0]
-    tile = 512
+    rows, tile = wide * tall * own, wide * own
     return pl.pallas_call(
         back_kernel,
         out_shape=[like((rows, feats)), TOKEN],
         grid=(rows // tile,),
         in_specs=[
             ANY,
-            pl.BlockSpec((tile, width), lambda i: (i, 0)),
+            pl.BlockSpec((wide, 1, own, width), lambda i: (0, i, 0, 0)),
             pl.BlockSpec((feats, width), lambda i: (0, 0)),
         ],
         out_specs=[pl.BlockSpec((tile, feats), lambda i: (i, 0)), pl.BlockSpec((8, 128), lambda i: (0, 0))],
@@ -206,16 +211,16 @@
 def local(tokens, key_grad, weight, moment, second):
     rows, width, feats = tokens.shape[0], key_grad.shape[1], tokens.shape[1]
     size = lax.axis_size
-    piece = swap_parts(copies_of(key_grad, size("zl") * size("x")), BLK).reshape(rows, width)
-
-    grad = lax.dot_general(tokens, piece, (((0,), (0,)), ((), ())), preferred_element_type=F32) * FACTOR
+    piece = swap_parts(copies_of(key_grad, size("zl") * size("x")), CROSS).reshape(rows, width)
+
+    held, own, *out = partial_keys(tokens, weight, size("x"))
+    grad = lax.dot_general(held, piece, (((0,), (0,)), ((), ())), preferred_element_type=F32) * FACTOR
     grad = grad.astype(BF16)
-    own, *out = partial_keys(tokens, weight, size("x"))
     got = [send(x, "x", 1 + i) for i, x in enumerate(out)]
     pair = pair_sum(grad, got[0])
     shares = swap_parts(pair.reshape(size("y"), -1, width), "y")
     shares, first = sum_copies(shares, size("zh"))
-    back, after_back = token_gradient(piece, weight, first)
+    back, after_back = token_gradient(piece.reshape(size("x"), size("zl"), -1, width), weight, first)
     mine, *out, after_keys = ring_sum([own] + got, first)
     got = [send(x, "zl", 1 + i) for i, x in enumerate(out)]
     shares, _ = sum_copies(swap_parts(shares, "zh"), size("y"), after_back, after_keys)

time: 112 us -> 112 us (level)
  blocking collectives: 19.6 us -> 14.1 us
  starting transfers between devices: 46.5 us -> 48.4 us
  waiting for transfers between devices: 24.8 us -> 26.7 us
  local copies, waits for them, and re-layouts: 6.35 us -> 7.53 us
    all_gather x1, blocking collectives: 13.8 us -> 8.78 us  [pair_sum(): lax.all_gather(lax.dynamic_slice_in_dim(grad, (1 - core) * rows, rows, 0)...]
    all_to_all x4, waiting for transfers between devices: 24.8 us -> 26.6 us  [swap_parts(): return lax.all_to_all(x, axes, 0, 0, tiled=True)]
    unnamed x18 -> x20, local copies, waits for them, and re-layouts: 6.33 us -> 7.5 us
    all_to_all x4, starting transfers between devices: 31.4 us -> 32.5 us  [swap_parts(): return lax.all_to_all(x, axes, 0, 0, tiled=True)]
  transfers between devices with their start and end apart: 9 -> 9, of which waited for: 4 -> 4; matrix products, arithmetic and copies ran while one was open for 6% -> 6% of each run, Pallas kernels for 4% -> 5%
where the time goes in v4:
time: 112 us; the launch traced here: 111 us
  starting transfers between devices  48.4 us (43%)
  waiting for transfers between devices  26.7 us (24%)
  blocking collectives  14.1 us (13%)
  local copies, waits for them, and re-layouts  7.53 us (7%)
  Pallas kernels  7.41 us (7%)
  other arithmetic  3.92 us (4%)
  matrix products  2.41 us (2%)
    all_to_all x4, starting transfers between devices, swap_parts(): return lax.all_to_all(x, axes, 0, 0, tiled=True)  32.5 us
    all_to_all x4, waiting for transfers between devices, swap_parts(): return lax.all_to_all(x, axes, 0, 0, tiled=True)  26.6 us
    ppermute x5, starting transfers between devices, send(): lax.ppermute(x, axis, [(i, (i + shift) % count) for i in range(count)])  15.9 us
    all_gather x1, blocking collectives, pair_sum(): lax.all_gather(lax.dynamic_slice_in_dim(grad, (1 - core) * rows, rows, 0)...  8.78 us
    unnamed x20, local copies, waits for them, and re-layouts  7.5 us
    all_gather x1, blocking collectives, local(): weight_grad = lax.all_gather(half, 'c', axis=0, tiled=True).astype(F32)  5.29 us
    sub x1, other arithmetic, optimize(): weight_new = weight - 0.05 * (step_dir + 0.1 * weight)  3.92 us
    pallas_call x1, Pallas kernels, token_gradient(): pl.pallas_call(back_kernel, out_shape=[like((rows, feats)), TOKEN], grid=...  2.7 us
  transfers between devices with their start and end apart: 9, of which 4 were waited for; matrix products, arithmetic and copies ran while one was open for 6% of the time, Pallas kernels for 5%

profile of v4, /device:TPU:1, one launch (start us, length us, event | category | flops | bytes accessed | tf_op | source)
XLA Modules:
  0.0 111.2 jit_solution(12559145194123131174)
XLA Ops:
  0.6 0.9 copy-done.7
  1.5 0.1 shard_map.101
  1.7 1.2 %copy-done.1 = bf16[12,128,512]{2,1,0:T(8,128)(2,1)} copy-done((bf16[12,128,512]{2,1,0:T(8,128)(2,1)}, bf16[12,128,512]{2,1,0:T(8,128)(2,1)S(1)}, u32[]{:S(2)}) %copy-start.1) | copy-done | bytes 1572888
  2.8 8.6 %all-to-all-start = ((bf16[12,128,512]{2,1,0:T(8,128)(2,1)}), bf16[12,128,512]{2,1,0:T(8,128)(2,1)S(1)}, u32[]{:S(2)}, u32[]{:S(2)}) async-start(bf16[12,128,512]{2,1,0:T(8,128)(2,1)} %copy-done.1), calls=%async_computation | async-start | bytes 3145728 | tf_op jit(solution)/shard_map/all_to_all | solution.py:44
  11.5 1.4 %copy-done.3 = bf16[1536,512]{1,0:T(8,128)(2,1)S(1)} copy-done((bf16[1536,512]{1,0:T(8,128)(2,1)S(1)}, bf16[1536,512]{1,0:T(8,128)(2,1)}, u32[]{:S(2)}) %copy-start.3) | copy-done | bytes 1572888
  12.9 1.1 shard_map.100
  14.0 1.1 %copy-done.2 = bf16[1536,512]{1,0:T(8,128)(2,1)} copy-done((bf16[1536,512]{1,0:T(8,128)(2,1)}, bf16[1536,512]{1,0:T(8,128)(2,1)S(1)}, u32[]{:S(2)}) %copy-start.2) | copy-done | bytes 1572888
  15.1 0.7 copy-done.4
  15.9 0.7 copy-done.8
  16.6 0.7 copy-done.9
  17.4 3.3 %collective-permute-start = (bf16[384,512]{1,0:T(8,128)(2,1)S(1)}, bf16[384,512]{1,0:T(8,128)(2,1)S(1)}, u32[]{:S(2)}, u32[]{:S(2)}) collective-permute-start(bf16[384,512]{1,0:T(8,128)(2,1)S(1)} %get-tuple-element.21), channel_id=1, source_target_pairs={{0,1},{1,2},{2,3},{3,0},{4,5},{5,6},{6,7},{7,4},{8,9},{9,10},{10,1... | collective-permute-start | bytes 1179656 | tf_op jit(solution)/shard_map/ppermute | solution.py:177
  20.7 12.2 %all-to-all-done = bf16[12,128,512]{2,1,0:T(8,128)(2,1)S(1)} async-done(((bf16[12,128,512]{2,1,0:T(8,128)(2,1)}), bf16[12,128,512]{2,1,0:T(8,128)(2,1)S(1)}, u32[]{:S(2)}, u32[]{:S(2)}) %all-to-all-start) | async-done | bytes 1572896 | tf_op jit(solution)/shard_map/all_to_all | solution.py:44
  32.8 2.4 %fusion.grad_ref = bf16[512,512]{1,0:T(8,128)(2,1)S(1)} fusion(bf16[1536,512]{1,0:T(8,128)(2,1)} %copy-done.2, bf16[1536,512]{1,0:T(8,128)(2,1)S(1)} %bitcast.10), kind=kOutput, calls=%fused_computation.2 | convolution fusion | flops 805830656 | bytes 3670016 | tf_op jit(solution)/shard_map/dot_general | solution.py:217
  35.3 8.8 %all-gather = bf16[512,512]{1,0:T(8,128)(2,1)S(1)} all-gather(bf16[256,512]{1,0:T(8,128)(2,1)S(1)} %constant_dynamic-slice_fusion), channel_id=2, replica_groups=mesh['y'=8,'zh'=4,'c'=2,'zl'=3,'x'=4] {'c'}, dimensions={0}, use_global_device_ids=true | all-gather | bytes 786432 | tf_op jit(solution)/shard_map/all_gather | solution.py:149
  44.1 0.8 shard_map.102
  44.8 6.8 %all-to-all-start.1 = ((bf16[8,32,512]{2,1,0:T(8,128)(2,1)}), bf16[8,32,512]{2,1,0:T(8,128)(2,1)S(1)}, u32[]{:S(2)}, u32[]{:S(2)}) async-start(bf16[8,32,512]{2,1,0:T(8,128)(2,1)} %bitcast.5), calls=%async_computation.1 | async-start | bytes 524288 | tf_op jit(solution)/shard_map/all_to_all | solution.py:44
  51.6 2.2 %collective-permute-start.1 = (bf16[384,512]{1,0:T(8,128)(2,1)}, bf16[384,512]{1,0:T(8,128)(2,1)}, u32[]{:S(2)}, u32[]{:S(2)}) collective-permute-start(bf16[384,512]{1,0:T(8,128)(2,1)} %copy-done.9), channel_id=1, source_target_pairs={{0,2},{1,3},{2,0},{3,1},{4,6},{5,7},{6,4},{7,5},{8,10},{9,11},{10,... | collective-permute-start | bytes 1179656 | tf_op jit(solution)/shard_map/ppermute | solution.py:177
  53.8 4.2 %collective-permute-start.2 = (bf16[384,512]{1,0:T(8,128)(2,1)}, bf16[384,512]{1,0:T(8,128)(2,1)}, u32[]{:S(2)}, u32[]{:S(2)}) collective-permute-start(bf16[384,512]{1,0:T(8,128)(2,1)} %copy-done.8), channel_id=1, source_target_pairs={{0,3},{1,0},{2,1},{3,2},{4,7},{5,4},{6,5},{7,6},{8,11},{9,8},{10,9... | collective-permute-start | bytes 1179656 | tf_op jit(solution)/shard_map/ppermute | solution.py:177
  58.0 4.7 %all-to-all-done.1.x_ref = bf16[8,32,512]{2,1,0:T(8,128)(2,1)S(1)} async-done(((bf16[8,32,512]{2,1,0:T(8,128)(2,1)}), bf16[8,32,512]{2,1,0:T(8,128)(2,1)S(1)}, u32[]{:S(2)}, u32[]{:S(2)}) %all-to-all-start.1) | async-done | bytes 262176 | tf_op jit(solution)/shard_map/all_to_all | solution.py:44
  62.7 0.6 copy-done.6
  63.4 13.7 %all-to-all-start.2 = ((bf16[4,32,512]{2,1,0:T(8,128)(2,1)}), bf16[4,32,512]{2,1,0:T(8,128)(2,1)S(1)}, u32[]{:S(2)}, u32[]{:S(2)}) async-start(bf16[4,32,512]{2,1,0:T(8,128)(2,1)} %copy-done.6), calls=%async_computation.2 | async-start | bytes 262144 | tf_op jit(solution)/shard_map/all_to_all | solution.py:44
  77.1 2.7 %shard_map.105 = (bf16[1536,512]{1,0:T(8,128)(2,1)}, f32[8,128]{1,0:T(8,128)S(1)}) custom-call(f32[8,128]{1,0:T(8,128)S(1)} %get-tuple-element.22.after_ref, bf16[4,3,128,512]{3,2,1,0:T(8,128)(2,1)S(1)} %bitcast.11, f32[512,512]{1,0:T(8,128)S(1)} %copy-done), custom_call_target="tpu_custom_call" | custom-call | flops 1 | bytes 1 | tf_op jit(solution)/shard_map/pallas_call | solution.py:195
  79.8 1.3 %shard_map.104 = (f32[128,512]{1,0:T(8,128)S(1)}, bf16[128,512]{1,0:T(8,128)(2,1)S(1)}, bf16[128,512]{1,0:T(8,128)(2,1)S(1)}, f32[8,128]{1,0:T(8,128)S(1)}) custom-call(s32[1]{0:T(128)} %bitcast.me_ref, f32[8,128]{1,0:T(8,128)S(1)} %get-tuple-element.22.after_ref, bf16[384,512]{1,0:T(8,128)(2,1)S(1)} %copy-done.5, ...), custom_call_target="tpu_custom_call" | custom-call | flops 1 | bytes 1 | tf_op jit(solution)/shard_map/pallas_call | solution.py:129
  81.1 6.6 %all-to-all-done.2.x_ref = bf16[4,32,512]{2,1,0:T(8,128)(2,1)S(1)} async-done(((bf16[4,32,512]{2,1,0:T(8,128)(2,1)}), bf16[4,32,512]{2,1,0:T(8,128)(2,1)S(1)}, u32[]{:S(2)}, u32[]{:S(2)}) %all-to-all-start.2) | async-done | bytes 131104 | tf_op jit(solution)/shard_map/all_to_all | solution.py:44
  87.8 0.7 shard_map.106
  88.5 3.4 %all-to-all-start.3 = ((bf16[8,32,512]{2,1,0:T(8,128)(2,1)}), bf16[8,32,512]{2,1,0:T(8,128)(2,1)S(1)}, u32[]{:S(2)}, u32[]{:S(2)}) async-start(bf16[8,32,512]{2,1,0:T(8,128)(2,1)} %get-tuple-element.32), calls=%async_computation.3 | async-start | bytes 524288 | tf_op jit(solution)/shard_map/all_to_all | solution.py:44
  91.9 2.6 %collective-permute-start.3 = (bf16[128,512]{1,0:T(8,128)(2,1)S(1)}, bf16[128,512]{1,0:T(8,128)(2,1)S(1)}, u32[]{:S(2)}, u32[]{:S(2)}) collective-permute-start(bf16[128,512]{1,0:T(8,128)(2,1)S(1)} %get-tuple-element.27), channel_id=1, source_target_pairs={{0,4},{4,8},{8,0},{1,5},{5,9},{9,1},{2,6},{6,10},{10,2},{3,7},{7,1... | collective-permute-start | bytes 393224 | tf_op jit(solution)/shard_map/ppermute | solution.py:177
  94.5 3.6 %collective-permute-start.4 = (bf16[128,512]{1,0:T(8,128)(2,1)S(1)}, bf16[128,512]{1,0:T(8,128)(2,1)S(1)}, u32[]{:S(2)}, u32[]{:S(2)}) collective-permute-start(bf16[128,512]{1,0:T(8,128)(2,1)S(1)} %get-tuple-element.28), channel_id=1, source_target_pairs={{0,8},{4,0},{8,4},{1,9},{5,1},{9,5},{2,10},{6,2},{10,6},{3,11},{7,... | collective-permute-start | bytes 393224 | tf_op jit(solution)/shard_map/ppermute | solution.py:177
  98.1 3.2 %all-to-all-done.3 = bf16[8,32,512]{2,1,0:T(8,128)(2,1)S(1)} async-done(((bf16[8,32,512]{2,1,0:T(8,128)(2,1)}), bf16[8,32,512]{2,1,0:T(8,128)(2,1)S(1)}, u32[]{:S(2)}, u32[]{:S(2)}) %all-to-all-start.3) | async-done | bytes 262176 | tf_op jit(solution)/shard_map/all_to_all | solution.py:44
  101.3 5.3 %all_gather.11 = bf16[512,512]{1,0:T(8,128)(2,1)S(1)} all-gather(bf16[256,512]{1,0:T(8,128)(2,1)S(1)} %bitcast.12), channel_id=1, replica_groups=mesh['y'=8,'zh'=4,'c'=2,'zl'=3,'x'=4] {'c'}, dimensions={0}, use_global_device_ids=true | all-gather | bytes 786432 | tf_op jit(solution)/shard_map/all_gather | solution.py:228
  106.6 3.9 %multiply_subtract_fusion = (f32[512,512]{1,0:T(8,128)}, f32[512,512]{1,0:T(8,128)}, f32[512,512]{1,0:T(8,128)}, f32[512,512]{1,0:T(8,128)}) fusion(f32[512,512]{1,0:T(8,128)S(1)} %copy-done, f32[512,512]{1,0:T(8,128)} %param.8, f32[512,512]{1,0:T(8,128)} %param.9, bf16[512,512]{1,0:T(8,128)(2,1)S(1)} %all_gather.11), kind=kLoop, calls=%fused_computation.4 | loop fusion | flops 4194304 | bytes 7864320 | tf_op jit(solution)/shard_map/sub | solution.py:28
  110.5 0.7 shard_map.107
  (19 shorter events, 0.1 us)
Async XLA Ops:
  0.6 0.9 copy-start.7
  1.6 1.2 %copy-start.1 = (bf16[12,128,512]{2,1,0:T(8,128)(2,1)}, bf16[12,128,512]{2,1,0:T(8,128)(2,1)S(1)}, u32[]{:S(2)}) copy-start(bf16[12,128,512]{2,1,0:T(8,128)(2,1)S(1)} %shard_map.101) | copy-start | bytes 4718596
  2.8 8.6 %copy-start = (f32[512,512]{1,0:T(8,128)S(1)}, f32[512,512]{1,0:T(8,128)}, u32[]{:S(2)}) copy-start(f32[512,512]{1,0:T(8,128)} %weight_ref.3) | copy-start | bytes 3145732
  2.8 30.0 %all-to-all-start = ((bf16[12,128,512]{2,1,0:T(8,128)(2,1)}), bf16[12,128,512]{2,1,0:T(8,128)(2,1)S(1)}, u32[]{:S(2)}, u32[]{:S(2)}) async-start(bf16[12,128,512]{2,1,0:T(8,128)(2,1)} %copy-done.1), calls=%async_computation | async-start | bytes 3145728 | tf_op jit(solution)/shard_map/all_to_all | solution.py:44
  11.5 1.4 %copy-start.3 = (bf16[1536,512]{1,0:T(8,128)(2,1)S(1)}, bf16[1536,512]{1,0:T(8,128)(2,1)}, u32[]{:S(2)}) copy-start(bf16[1536,512]{1,0:T(8,128)(2,1)} %tokens_ref.1) | copy-start | bytes 4718596
  14.0 1.1 %copy-start.2 = (bf16[1536,512]{1,0:T(8,128)(2,1)}, bf16[1536,512]{1,0:T(8,128)(2,1)S(1)}, u32[]{:S(2)}) copy-start(bf16[1536,512]{1,0:T(8,128)(2,1)S(1)} %get-tuple-element.20) | copy-start | bytes 4718596
  15.1 0.7 copy-start.4
  15.9 0.7 copy-start.8
  16.6 0.7 copy-start.9
  17.4 26.7 %collective-permute-start = (bf16[384,512]{1,0:T(8,128)(2,1)S(1)}, bf16[384,512]{1,0:T(8,128)(2,1)S(1)}, u32[]{:S(2)}, u32[]{:S(2)}) collective-permute-start(bf16[384,512]{1,0:T(8,128)(2,1)S(1)} %get-tuple-element.21), channel_id=1, source_target_pairs={{0,1},{1,2},{2,3},{3,0},{4,5},{5,6},{6,7},{7,4},{8,9},{9,10},{10,1... | collective-permute-start | bytes 1179656 | tf_op jit(solution)/shard_map/ppermute | solution.py:177
  44.8 17.9 %all-to-all-start.1 = ((bf16[8,32,512]{2,1,0:T(8,128)(2,1)}), bf16[8,32,512]{2,1,0:T(8,128)(2,1)S(1)}, u32[]{:S(2)}, u32[]{:S(2)}) async-start(bf16[8,32,512]{2,1,0:T(8,128)(2,1)} %bitcast.5), calls=%async_computation.1 | async-start | bytes 524288 | tf_op jit(solution)/shard_map/all_to_all | solution.py:44
  51.6 28.2 %collective-permute-start.1 = (bf16[384,512]{1,0:T(8,128)(2,1)}, bf16[384,512]{1,0:T(8,128)(2,1)}, u32[]{:S(2)}, u32[]{:S(2)}) collective-permute-start(bf16[384,512]{1,0:T(8,128)(2,1)} %copy-done.9), channel_id=1, source_target_pairs={{0,2},{1,3},{2,0},{3,1},{4,6},{5,7},{6,4},{7,5},{8,10},{9,11},{10,... | collective-permute-start | bytes 1179656 | tf_op jit(solution)/shard_map/ppermute | solution.py:177
  53.8 26.0 %collective-permute-start.2 = (bf16[384,512]{1,0:T(8,128)(2,1)}, bf16[384,512]{1,0:T(8,128)(2,1)}, u32[]{:S(2)}, u32[]{:S(2)}) collective-permute-start(bf16[384,512]{1,0:T(8,128)(2,1)} %copy-done.8), channel_id=1, source_target_pairs={{0,3},{1,0},{2,1},{3,2},{4,7},{5,4},{6,5},{7,6},{8,11},{9,8},{10,9... | collective-permute-start | bytes 1179656 | tf_op jit(solution)/shard_map/ppermute | solution.py:177
  62.7 0.7 copy-start.6
  63.4 16.4 %copy-start.5 = (bf16[384,512]{1,0:T(8,128)(2,1)S(1)}, bf16[384,512]{1,0:T(8,128)(2,1)}, u32[]{:S(2)}) copy-start(bf16[384,512]{1,0:T(8,128)(2,1)} %copy-done.4) | copy-start | bytes 1179652
  63.4 24.4 %all-to-all-start.2 = ((bf16[4,32,512]{2,1,0:T(8,128)(2,1)}), bf16[4,32,512]{2,1,0:T(8,128)(2,1)S(1)}, u32[]{:S(2)}, u32[]{:S(2)}) async-start(bf16[4,32,512]{2,1,0:T(8,128)(2,1)} %copy-done.6), calls=%async_computation.2 | async-start | bytes 262144 | tf_op jit(solution)/shard_map/all_to_all | solution.py:44
  88.5 12.8 %all-to-all-start.3 = ((bf16[8,32,512]{2,1,0:T(8,128)(2,1)}), bf16[8,32,512]{2,1,0:T(8,128)(2,1)S(1)}, u32[]{:S(2)}, u32[]{:S(2)}) async-start(bf16[8,32,512]{2,1,0:T(8,128)(2,1)} %get-tuple-element.32), calls=%async_computation.3 | async-start | bytes 524288 | tf_op jit(solution)/shard_map/all_to_all | solution.py:44
  91.9 18.6 %collective-permute-start.3 = (bf16[128,512]{1,0:T(8,128)(2,1)S(1)}, bf16[128,512]{1,0:T(8,128)(2,1)S(1)}, u32[]{:S(2)}, u32[]{:S(2)}) collective-permute-start(bf16[128,512]{1,0:T(8,128)(2,1)S(1)} %get-tuple-element.27), channel_id=1, source_target_pairs={{0,4},{4,8},{8,0},{1,5},{5,9},{9,1},{2,6},{6,10},{10,2},{3,7},{7,1... | collective-permute-start | bytes 393224 | tf_op jit(solution)/shard_map/ppermute | solution.py:177
  94.5 16.0 %collective-permute-start.4 = (bf16[128,512]{1,0:T(8,128)(2,1)S(1)}, bf16[128,512]{1,0:T(8,128)(2,1)S(1)}, u32[]{:S(2)}, u32[]{:S(2)}) collective-permute-start(bf16[128,512]{1,0:T(8,128)(2,1)S(1)} %get-tuple-element.28), channel_id=1, source_target_pairs={{0,8},{4,0},{8,4},{1,9},{5,1},{9,5},{2,10},{6,2},{10,6},{3,11},{7,... | collective-permute-start | bytes 393224 | tf_op jit(solution)/shard_map/ppermute | solution.py:177
